TPU v7x, 32 devices: a whole 2x2x4 slice. The times are simulated.
32 devices in a mesh: gx: 4 (over z), gy: 2 (over y), gz: 4 (over x, core).
Axes of the slice: x: 2, y: 2, z: 4, core: 2. Of those that a mesh axis runs over, the one named last changes fastest.
Arguments:
- fields: float32 [4, 32, 64, 512], P(None, 'gx', 'gy', 'gz'), may hold values from -6 to 6
- velocity: float32 [3, 32, 64, 512], P(None, 'gx', 'gy', 'gz'), may hold values from -3 to 3
- diffusivity: float32 [4], replicated, may hold values from 0.05 to 0.5
- coupling: float32 [4, 4], replicated, may hold values from -1 to 1
- factor_x: float32 [32, 32], P('gx'), may hold values from -1 to 1, as said below
- factor_y: float32 [64, 32], P('gy'), may hold values from -1 to 1, as said below
- factor_z: float32 [512, 32], P('gz'), may hold values from -1 to 1, as said below
Outputs:
- core_tensor: float32 [4, 32, 32, 32], P(None, 'gx', 'gy', 'gz')
Inputs may be any that keep to these rules, and one draw needn't show every extreme that they name: `factor_x`: the columns of each factor are orthonormal. `factor_y`: the columns of each factor are orthonormal. `factor_z`: the columns of each factor are orthonormal.
All inputs are finite; a program needn't handle non-finite values.
Results may differ from a plain program's by a relative error of at most 0.0003.
Values sent between devices are 32-bit elements; how exact they have to be, the bound alone decides.
A program may use at most 64 MiB of HBM per device.

v0:
```python
import jax
import jax.numpy as jnp
from jax import lax
from jax.sharding import PartitionSpec as P

STEPS = 2


time_step = 0.2


def with_halo(cells, sides, width):
    for axis, dim in sides:
        count = lax.axis_size(axis)
        ends = count - 1
        head = lax.slice_in_dim(cells, 0, width, axis=dim)
        tail = lax.slice_in_dim(cells, cells.shape[dim] - width, cells.shape[dim], axis=dim)
        cells = jnp.concatenate(
            [
                lax.ppermute(tail, axis, [(i, (i + 1) % count) for i in range(ends)]),
                cells,
                lax.ppermute(head, axis, [((i + 1) % count, i) for i in range(ends)]),
            ],
            axis=dim,
        )
    return cells


def offset_view(padded, dimension, offset):
    indices = [slice(None)]
    for other in (1, 2, 3):
        if other == dimension:
            first_cell = 2 + offset
            indices.append(slice(first_cell, first_cell + padded.shape[other] - 4))
        else:
            indices.append(slice(2, padded.shape[other] - 2))
    return padded[tuple(indices)]


def tendency(padded, velocity, diffusivity, coupling):
    center = offset_view(padded, 1, 0)
    transport = jnp.zeros_like(center)
    laplace = jnp.zeros_like(center)
    for dimension in (1, 2, 3):
        gradient = (
            8.0 * (offset_view(padded, dimension, 1) - offset_view(padded, dimension, -1))
            - (offset_view(padded, dimension, 2) - offset_view(padded, dimension, -2))
        ) / 12.0
        transport = transport + velocity[dimension - 1][None] * gradient
        laplace = (
            laplace
            + offset_view(padded, dimension, 1)
            + offset_view(padded, dimension, -1)
            - 2.0 * center
        )
    mixing = jnp.einsum("vw,wxyz->vxyz", coupling, center, precision=lax.Precision.HIGHEST)
    return -transport + diffusivity[:, None, None, None] * laplace + center * mixing


def with_edges(values):
    return with_halo(values, (("gx", 1), ("gy", 2), ("gz", 3)), 2)


def local(fields, velocity, diffusivity, coupling, factor_x, factor_y, factor_z):
    state = fields
    for repeat in range(STEPS):
        section = state + time_step * tendency(with_edges(state), velocity, diffusivity, coupling)
        state = 0.5 * (
            state
            + section
            + time_step * tendency(with_edges(section), velocity, diffusivity, coupling)
        )
    highest = lax.Precision.HIGHEST
    partial_value = jnp.einsum("vxyz,zc->vxyc", state, factor_z, precision=highest)
    partial_value = lax.psum_scatter(partial_value, "gz", scatter_dimension=3, tiled=True)
    partial_value = jnp.einsum("vxyc,yb->vxbc", partial_value, factor_y, precision=highest)
    partial_value = lax.psum_scatter(partial_value, "gy", scatter_dimension=2, tiled=True)
    partial_value = jnp.einsum("vxbc,xa->vabc", partial_value, factor_x, precision=highest)
    core_tensor = lax.psum_scatter(partial_value, "gx", scatter_dimension=1, tiled=True)
    return core_tensor


def solution(mesh):
    return jax.shard_map(
        local,
        mesh=mesh,
        in_specs=(
            P(None, "gx", "gy", "gz"),
            P(None, "gx", "gy", "gz"),
            P(),
            P(),
            P("gx", None),
            P("gy", None),
            P("gz", None),
        ),
        out_specs=P(None, "gx", "gy", "gz"),
        check_vma=False,
    )
```

profile of v0, /device:TPU:0, one launch (start us, length us, event | category | flops | bytes accessed | tf_op | source)
XLA Modules:
  0.0 213.4 jit_solution(14649650723848805642)
XLA Ops:
  7.6 5.1 %collective-permute-start.1 = (f32[4,2,32,128]{3,0,2,1:T(4,128)S(1)}, f32[4,2,32,128]{3,0,2,1:T(4,128)S(1)}, u32[]{:S(2)}, u32[]{:S(2)}) collective-permute-start(f32[4,2,32,128]{3,0,2,1:T(4,128)S(1)} %copy.68), channel_id=1, source_target_pairs={{0,8},{8,16},{16,24},{1,9},{9,17},{17,25},{2,10},{10,18},{18,26},{... | collective-permute-start | bytes 393224 | tf_op jit(solution)/shard_map/ppermute | solution.py:20
  16.1 3.6 %collective-permute-done = f32[4,2,32,128]{3,0,2,1:T(4,128)S(1)} collective-permute-done((f32[4,2,32,128]{3,0,2,1:T(4,128)S(1)}, f32[4,2,32,128]{3,0,2,1:T(4,128)S(1)}, u32[]{:S(2)}, u32[]{:S(2)}) %collective-permute-start) | collective-permute-done | bytes 131104 | tf_op jit(solution)/shard_map/ppermute | solution.py:22
  19.8 3.4 %collective-permute-start.3 = (f32[4,12,2,128]{3,0,2,1:T(4,128)S(1)}, f32[4,12,2,128]{3,0,2,1:T(4,128)S(1)}, u32[]{:S(2)}, u32[]{:S(2)}) collective-permute-start(f32[4,12,2,128]{3,0,2,1:T(4,128)S(1)} %get-tuple-element.25), channel_id=1, source_target_pairs={{0,4},{1,5},{2,6},{3,7},{8,12},{9,13},{10,14},{11,15},{16,20},{17,... | collective-permute-start | bytes 147464 | tf_op jit(solution)/shard_map/ppermute | solution.py:20
  24.9 4.3 %collective-permute-done.2 = f32[4,12,2,128]{3,0,2,1:T(4,128)S(1)} collective-permute-done((f32[4,12,2,128]{3,0,2,1:T(4,128)S(1)}, f32[4,12,2,128]{3,0,2,1:T(4,128)S(1)}, u32[]{:S(2)}, u32[]{:S(2)}) %collective-permute-start.2) | collective-permute-done | bytes 49184 | tf_op jit(solution)/shard_map/ppermute | solution.py:22
  33.5 3.5 %collective-permute-done.4 = f32[4,12,36,2]{2,0,3,1:T(4,128)S(1)} collective-permute-done((f32[4,12,36,2]{2,0,3,1:T(4,128)S(1)}, f32[4,12,36,2]{2,0,3,1:T(4,128)S(1)}, u32[]{:S(2)}, u32[]{:S(2)}) %collective-permute-start.4) | collective-permute-done | bytes 13856 | tf_op jit(solution)/shard_map/ppermute | solution.py:22
  40.5 5.2 %fusion.2 = f32[4,8,32,128]{3,0,2,1:T(4,128)S(1)} fusion(f32[4,12,36,2]{3,0,2,1:T(4,128)} %copy.27, f32[4,12,2,128]{3,0,2,1:T(4,128)S(1)} %collective-permute-done.2, f32[4,12,32,128]{3,0,2,1:T(4,128)S(1)} %get-tuple-element.42, f32[4,12,2,128]{3,0,2,1:T(4,128)S(1)} %collective-permute-done.3, f32[4,12,36,2]{3,0,2,1:T(4,128)} %copy.25, ...), kind=kOutput, calls=%fused_computation.3 | convolution fusion | flops 12713984 | bytes 4978176 | tf_op jit(solution)/shard_map/vw,wxyz->vxyz/dot_general | solution.py:56
  45.7 3.5 %collective-permute-start.7 = (f32[4,2,32,128]{3,0,2,1:T(4,128)S(1)}, f32[4,2,32,128]{3,0,2,1:T(4,128)S(1)}, u32[]{:S(2)}, u32[]{:S(2)}) collective-permute-start(f32[4,2,32,128]{3,0,2,1:T(4,128)S(1)} %get-tuple-element.31), channel_id=1, source_target_pairs={{0,8},{8,16},{16,24},{1,9},{9,17},{17,25},{2,10},{10,18},{18,26},{... | collective-permute-start | bytes 393224 | tf_op jit(solution)/shard_map/ppermute | solution.py:20
  51.7 4.4 %collective-permute-done.6 = f32[4,2,32,128]{3,0,2,1:T(4,128)S(1)} collective-permute-done((f32[4,2,32,128]{3,0,2,1:T(4,128)S(1)}, f32[4,2,32,128]{3,0,2,1:T(4,128)S(1)}, u32[]{:S(2)}, u32[]{:S(2)}) %collective-permute-start.6) | collective-permute-done | bytes 131104 | tf_op jit(solution)/shard_map/ppermute | solution.py:22
  56.1 1.6 collective-permute-start.9
  59.5 4.6 %collective-permute-done.8 = f32[4,12,2,128]{3,0,2,1:T(4,128)S(1)} collective-permute-done((f32[4,12,2,128]{3,0,2,1:T(4,128)S(1)}, f32[4,12,2,128]{3,0,2,1:T(4,128)S(1)}, u32[]{:S(2)}, u32[]{:S(2)}) %collective-permute-start.8) | collective-permute-done | bytes 49184 | tf_op jit(solution)/shard_map/ppermute | solution.py:22
  65.7 2.0 collective-permute-start.11
  70.4 2.1 collective-permute-done.10
  74.5 6.0 %broadcast_multiply_fusion = (f32[4,8,32,128]{3,0,2,1:T(4,128)S(1)}, f32[4,8,32,128]{3,0,2,1:T(4,128)}) fusion(f32[4,8,32,128]{3,0,2,1:T(4,128)S(1)} %fusion.2, f32[4,4]{1,0:T(4,128)S(1)} %copy-done.18, f32[4]{0:T(128)S(1)} %copy-done.21, f32[8,32,128]{2,1,0:T(8,128)S(1)} %get-tuple-element.39, f32[4,12,2,128]{3,0,2,1:T(4,128)S(1)} %collective-permute-done.8, ...), kind=kOutput, calls=%fused_computation.172 | convolution fusion | flops 14024704 | bytes 6373376 | tf_op jit(solution)/shard_map/vw,wxyz->vxyz/dot_general | solution.py:56
  80.5 3.5 %collective-permute-start.13 = (f32[4,2,32,128]{3,0,2,1:T(4,128)S(1)}, f32[4,2,32,128]{3,0,2,1:T(4,128)S(1)}, u32[]{:S(2)}, u32[]{:S(2)}) collective-permute-start(f32[4,2,32,128]{3,0,2,1:T(4,128)S(1)} %get-tuple-element.29), channel_id=1, source_target_pairs={{0,8},{8,16},{16,24},{1,9},{9,17},{17,25},{2,10},{10,18},{18,26},{... | collective-permute-start | bytes 393224 | tf_op jit(solution)/shard_map/ppermute | solution.py:20
  86.5 4.4 %collective-permute-done.12 = f32[4,2,32,128]{3,0,2,1:T(4,128)S(1)} collective-permute-done((f32[4,2,32,128]{3,0,2,1:T(4,128)S(1)}, f32[4,2,32,128]{3,0,2,1:T(4,128)S(1)}, u32[]{:S(2)}, u32[]{:S(2)}) %collective-permute-start.12) | collective-permute-done | bytes 131104 | tf_op jit(solution)/shard_map/ppermute | solution.py:22
  90.9 1.6 collective-permute-start.15
  94.3 4.6 %collective-permute-done.14 = f32[4,12,2,128]{3,0,2,1:T(4,128)S(1)} collective-permute-done((f32[4,12,2,128]{3,0,2,1:T(4,128)S(1)}, f32[4,12,2,128]{3,0,2,1:T(4,128)S(1)}, u32[]{:S(2)}, u32[]{:S(2)}) %collective-permute-start.14) | collective-permute-done | bytes 49184 | tf_op jit(solution)/shard_map/ppermute | solution.py:22
  100.5 2.0 collective-permute-start.17
  104.0 1.5 pad_maximum_fusion.5
  105.5 1.9 collective-permute-done.16
  109.1 5.0 %fusion.9 = f32[4,8,32,128]{3,0,2,1:T(4,128)S(1)} fusion(f32[4,8,32,128]{3,0,2,1:T(4,128)S(1)} %get-tuple-element.45, f32[4,12,36,2]{3,0,2,1:T(4,128)S(1)} %copy.40, f32[4,12,2,128]{3,0,2,1:T(4,128)S(1)} %collective-permute-done.14, f32[4,12,2,128]{3,0,2,1:T(4,128)S(1)} %collective-permute-done.15, f32[4,2,32,128]{3,0,2,1:T(4,128)S(1)} %collective-permute-done.12, ...), kind=kOutput, calls=%fused_computation.12 | convolution fusion | flops 13631488 | bytes 6720000 | tf_op jit(solution)/shard_map/vw,wxyz->vxyz/dot_general | solution.py:56
  114.1 1.9 collective-permute-start.19
  118.5 4.4 %collective-permute-done.18 = f32[4,2,32,128]{3,0,2,1:T(4,128)S(1)} collective-permute-done((f32[4,2,32,128]{3,0,2,1:T(4,128)S(1)}, f32[4,2,32,128]{3,0,2,1:T(4,128)S(1)}, u32[]{:S(2)}, u32[]{:S(2)}) %collective-permute-start.18) | collective-permute-done | bytes 131104 | tf_op jit(solution)/shard_map/ppermute | solution.py:22
  122.9 1.6 collective-permute-start.21
  126.3 4.6 %collective-permute-done.20 = f32[4,12,2,128]{3,0,2,1:T(4,128)S(1)} collective-permute-done((f32[4,12,2,128]{3,0,2,1:T(4,128)S(1)}, f32[4,12,2,128]{3,0,2,1:T(4,128)S(1)}, u32[]{:S(2)}, u32[]{:S(2)}) %collective-permute-start.20) | collective-permute-done | bytes 49184 | tf_op jit(solution)/shard_map/ppermute | solution.py:22
  132.5 2.0 collective-permute-start.23
  137.4 2.1 collective-permute-done.22
  141.1 5.0 %fusion.15 = f32[4,8,32,128]{3,0,2,1:T(4,128)S(1)} fusion(f32[4,8,32,128]{3,0,2,1:T(4,128)S(1)} %fusion.9, f32[4,12,36,2]{3,0,2,1:T(4,128)S(1)} %copy.44, f32[4,12,2,128]{3,0,2,1:T(4,128)S(1)} %collective-permute-done.20, f32[4,12,2,128]{3,0,2,1:T(4,128)S(1)} %collective-permute-done.21, f32[4,2,32,128]{3,0,2,1:T(4,128)S(1)} %collective-permute-done.18, ...), kind=kOutput, calls=%fused_computation.19 | convolution fusion | flops 14155776 | bytes 6720000 | tf_op jit(solution)/shard_map/vw,wxyz->vxyz/dot_general | solution.py:56
  148.0 20.3 %reduce-scatter.6.cloned.1.call-done = f32[4,8,32,8]{2,1,0,3:T(8,128)} async-done(((f32[4,8,32,32]{2,1,0,3:T(8,128)}), f32[4,8,32,8]{2,1,0,3:T(8,128)}) %reduce-scatter.6.cloned.1.call-update) | async-done | bytes 32784 | tf_op jit(solution)/shard_map/reduce_scatter | solution.py:75
  171.0 9.9 %reduce-scatter.10.cloned.1.call-done = f32[16,256]{1,0:T(8,128)} async-done(((f32[32,256]{1,0:T(8,128)}), f32[16,256]{1,0:T(8,128)}) %reduce-scatter.10.cloned.1.call-update) | async-done | bytes 16400
  183.5 21.8 %reduce-scatter.8.cloned.1.call-done = f32[4,8,16,8]{2,3,0,1:T(8,128)} async-done(((f32[4,32,16,8]{2,3,0,1:T(8,128)}), f32[4,8,16,8]{2,3,0,1:T(8,128)}) %reduce-scatter.8.cloned.1.call-update) | async-done | bytes 16400 | tf_op jit(solution)/shard_map/reduce_scatter | solution.py:79
  205.3 1.6 copy.46
  (127 shorter events, 51.0 us)
Async XLA Ops:
  6.5 139.6 %copy-start = (f32[128,32]{0,1:T(8,128)S(1)}, f32[128,32]{0,1:T(8,128)}, u32[]{:S(2)}) copy-start(f32[128,32]{0,1:T(8,128)} %param.13) | copy-start | bytes 49156
  6.5 161.8 %reduce-scatter.6.cloned.1.call-start = ((), (), s32[]{:S(2)}) async-start(), calls=%async_computation.3 | async-start | bytes 655360 | tf_op jit(solution)/shard_map/reduce_scatter | solution.py:75
  7.6 7.8 %collective-permute-start.1 = (f32[4,2,32,128]{3,0,2,1:T(4,128)S(1)}, f32[4,2,32,128]{3,0,2,1:T(4,128)S(1)}, u32[]{:S(2)}, u32[]{:S(2)}) collective-permute-start(f32[4,2,32,128]{3,0,2,1:T(4,128)S(1)} %copy.68), channel_id=1, source_target_pairs={{0,8},{8,16},{16,24},{1,9},{9,17},{17,25},{2,10},{10,18},{18,26},{... | collective-permute-start | bytes 393224 | tf_op jit(solution)/shard_map/ppermute | solution.py:20
  12.8 6.9 %collective-permute-start = (f32[4,2,32,128]{3,0,2,1:T(4,128)S(1)}, f32[4,2,32,128]{3,0,2,1:T(4,128)S(1)}, u32[]{:S(2)}, u32[]{:S(2)}) collective-permute-start(f32[4,2,32,128]{3,0,2,1:T(4,128)S(1)} %copy.69), channel_id=1, source_target_pairs={{8,0},{16,8},{24,16},{9,1},{17,9},{25,17},{10,2},{18,10},{26,18},{... | collective-permute-start | bytes 393224 | tf_op jit(solution)/shard_map/ppermute | solution.py:22
  16.0 13.1 %copy-start.15 = (f32[4,10,32,128]{3,0,2,1:T(4,128)}, f32[4,10,32,128]{3,0,2,1:T(4,128)S(1)}, u32[]{:S(2)}) copy-start(f32[4,10,32,128]{3,0,2,1:T(4,128)S(1)} %get-tuple-element.34) | copy-start | bytes 1966084
  19.8 5.2 %collective-permute-start.3 = (f32[4,12,2,128]{3,0,2,1:T(4,128)S(1)}, f32[4,12,2,128]{3,0,2,1:T(4,128)S(1)}, u32[]{:S(2)}, u32[]{:S(2)}) collective-permute-start(f32[4,12,2,128]{3,0,2,1:T(4,128)S(1)} %get-tuple-element.25), channel_id=1, source_target_pairs={{0,4},{1,5},{2,6},{3,7},{8,12},{9,13},{10,14},{11,15},{16,20},{17,... | collective-permute-start | bytes 147464 | tf_op jit(solution)/shard_map/ppermute | solution.py:20
  23.2 6.0 %collective-permute-start.2 = (f32[4,12,2,128]{3,0,2,1:T(4,128)S(1)}, f32[4,12,2,128]{3,0,2,1:T(4,128)S(1)}, u32[]{:S(2)}, u32[]{:S(2)}) collective-permute-start(f32[4,12,2,128]{3,0,2,1:T(4,128)S(1)} %get-tuple-element.26), channel_id=1, source_target_pairs={{4,0},{5,1},{6,2},{7,3},{12,8},{13,9},{14,10},{15,11},{20,16},{21,... | collective-permute-start | bytes 147464 | tf_op jit(solution)/shard_map/ppermute | solution.py:22
  30.8 7.6 %collective-permute-start.5 = (f32[4,12,36,2]{2,0,3,1:T(4,128)S(1)}, f32[4,12,36,2]{2,0,3,1:T(4,128)S(1)}, u32[]{:S(2)}, u32[]{:S(2)}) collective-permute-start(f32[4,12,36,2]{2,0,3,1:T(4,128)S(1)} %copy.26), channel_id=1, source_target_pairs={{0,1},{1,2},{2,3},{4,5},{5,6},{6,7},{8,9},{9,10},{10,11},{12,13},{... | collective-permute-start | bytes 41480 | tf_op jit(solution)/shard_map/ppermute | solution.py:20
  32.1 4.8 %collective-permute-start.4 = (f32[4,12,36,2]{2,0,3,1:T(4,128)S(1)}, f32[4,12,36,2]{2,0,3,1:T(4,128)S(1)}, u32[]{:S(2)}, u32[]{:S(2)}) collective-permute-start(f32[4,12,36,2]{2,0,3,1:T(4,128)S(1)} %copy.24), channel_id=1, source_target_pairs={{1,0},{2,1},{3,2},{5,4},{6,5},{7,6},{9,8},{10,9},{11,10},{13,12},{... | collective-permute-start | bytes 41480 | tf_op jit(solution)/shard_map/ppermute | solution.py:22
  33.5 41.0 %copy-start.6 = (f32[8,32,128]{2,1,0:T(8,128)}, f32[8,32,128]{2,1,0:T(8,128)S(1)}, u32[]{:S(2)}) copy-start(f32[8,32,128]{2,1,0:T(8,128)S(1)} %get-tuple-element.38) | copy-start | bytes 393220
  33.5 41.0 %copy-start.9 = (f32[8,32,128]{2,1,0:T(8,128)}, f32[8,32,128]{2,1,0:T(8,128)S(1)}, u32[]{:S(2)}) copy-start(f32[8,32,128]{2,1,0:T(8,128)S(1)} %get-tuple-element.39) | copy-start | bytes 393220
  45.7 6.0 %collective-permute-start.7 = (f32[4,2,32,128]{3,0,2,1:T(4,128)S(1)}, f32[4,2,32,128]{3,0,2,1:T(4,128)S(1)}, u32[]{:S(2)}, u32[]{:S(2)}) collective-permute-start(f32[4,2,32,128]{3,0,2,1:T(4,128)S(1)} %get-tuple-element.31), channel_id=1, source_target_pairs={{0,8},{8,16},{16,24},{1,9},{9,17},{17,25},{2,10},{10,18},{18,26},{... | collective-permute-start | bytes 393224 | tf_op jit(solution)/shard_map/ppermute | solution.py:20
  49.2 6.9 %collective-permute-start.6 = (f32[4,2,32,128]{3,0,2,1:T(4,128)S(1)}, f32[4,2,32,128]{3,0,2,1:T(4,128)S(1)}, u32[]{:S(2)}, u32[]{:S(2)}) collective-permute-start(f32[4,2,32,128]{3,0,2,1:T(4,128)S(1)} %get-tuple-element.32), channel_id=1, source_target_pairs={{8,0},{16,8},{24,16},{9,1},{17,9},{25,17},{10,2},{18,10},{26,18},{... | collective-permute-start | bytes 393224 | tf_op jit(solution)/shard_map/ppermute | solution.py:22
  56.1 3.4 %collective-permute-start.9 = (f32[4,12,2,128]{3,0,2,1:T(4,128)S(1)}, f32[4,12,2,128]{3,0,2,1:T(4,128)S(1)}, u32[]{:S(2)}, u32[]{:S(2)}) collective-permute-start(f32[4,12,2,128]{3,0,2,1:T(4,128)S(1)} %get-tuple-element.23), channel_id=1, source_target_pairs={{0,4},{1,5},{2,6},{3,7},{8,12},{9,13},{10,14},{11,15},{16,20},{17,... | collective-permute-start | bytes 147464 | tf_op jit(solution)/shard_map/ppermute | solution.py:20
  57.7 6.4 %collective-permute-start.8 = (f32[4,12,2,128]{3,0,2,1:T(4,128)S(1)}, f32[4,12,2,128]{3,0,2,1:T(4,128)S(1)}, u32[]{:S(2)}, u32[]{:S(2)}) collective-permute-start(f32[4,12,2,128]{3,0,2,1:T(4,128)S(1)} %get-tuple-element.24), channel_id=1, source_target_pairs={{4,0},{5,1},{6,2},{7,3},{12,8},{13,9},{14,10},{15,11},{20,16},{21,... | collective-permute-start | bytes 147464 | tf_op jit(solution)/shard_map/ppermute | solution.py:22
  65.7 7.4 %collective-permute-start.11 = (f32[4,12,36,2]{2,0,3,1:T(4,128)S(1)}, f32[4,12,36,2]{2,0,3,1:T(4,128)S(1)}, u32[]{:S(2)}, u32[]{:S(2)}) collective-permute-start(f32[4,12,36,2]{2,0,3,1:T(4,128)S(1)} %copy.35), channel_id=1, source_target_pairs={{0,1},{1,2},{2,3},{4,5},{5,6},{6,7},{8,9},{9,10},{10,11},{12,13},{... | collective-permute-start | bytes 41480 | tf_op jit(solution)/shard_map/ppermute | solution.py:20
  67.7 4.9 %collective-permute-start.10 = (f32[4,12,36,2]{2,0,3,1:T(4,128)S(1)}, f32[4,12,36,2]{2,0,3,1:T(4,128)S(1)}, u32[]{:S(2)}, u32[]{:S(2)}) collective-permute-start(f32[4,12,36,2]{2,0,3,1:T(4,128)S(1)} %copy.33), channel_id=1, source_target_pairs={{1,0},{2,1},{3,2},{5,4},{6,5},{7,6},{9,8},{10,9},{11,10},{13,12},{... | collective-permute-start | bytes 41480 | tf_op jit(solution)/shard_map/ppermute | solution.py:22
  80.5 6.0 %collective-permute-start.13 = (f32[4,2,32,128]{3,0,2,1:T(4,128)S(1)}, f32[4,2,32,128]{3,0,2,1:T(4,128)S(1)}, u32[]{:S(2)}, u32[]{:S(2)}) collective-permute-start(f32[4,2,32,128]{3,0,2,1:T(4,128)S(1)} %get-tuple-element.29), channel_id=1, source_target_pairs={{0,8},{8,16},{16,24},{1,9},{9,17},{17,25},{2,10},{10,18},{18,26},{... | collective-permute-start | bytes 393224 | tf_op jit(solution)/shard_map/ppermute | solution.py:20
  84.0 6.9 %collective-permute-start.12 = (f32[4,2,32,128]{3,0,2,1:T(4,128)S(1)}, f32[4,2,32,128]{3,0,2,1:T(4,128)S(1)}, u32[]{:S(2)}, u32[]{:S(2)}) collective-permute-start(f32[4,2,32,128]{3,0,2,1:T(4,128)S(1)} %get-tuple-element.30), channel_id=1, source_target_pairs={{8,0},{16,8},{24,16},{9,1},{17,9},{25,17},{10,2},{18,10},{26,18},{... | collective-permute-start | bytes 393224 | tf_op jit(solution)/shard_map/ppermute | solution.py:22
  90.9 3.4 %collective-permute-start.15 = (f32[4,12,2,128]{3,0,2,1:T(4,128)S(1)}, f32[4,12,2,128]{3,0,2,1:T(4,128)S(1)}, u32[]{:S(2)}, u32[]{:S(2)}) collective-permute-start(f32[4,12,2,128]{3,0,2,1:T(4,128)S(1)} %get-tuple-element.19), channel_id=1, source_target_pairs={{0,4},{1,5},{2,6},{3,7},{8,12},{9,13},{10,14},{11,15},{16,20},{17,... | collective-permute-start | bytes 147464 | tf_op jit(solution)/shard_map/ppermute | solution.py:20
  92.5 6.4 %collective-permute-start.14 = (f32[4,12,2,128]{3,0,2,1:T(4,128)S(1)}, f32[4,12,2,128]{3,0,2,1:T(4,128)S(1)}, u32[]{:S(2)}, u32[]{:S(2)}) collective-permute-start(f32[4,12,2,128]{3,0,2,1:T(4,128)S(1)} %get-tuple-element.20), channel_id=1, source_target_pairs={{4,0},{5,1},{6,2},{7,3},{12,8},{13,9},{14,10},{15,11},{20,16},{21,... | collective-permute-start | bytes 147464 | tf_op jit(solution)/shard_map/ppermute | solution.py:22
  100.5 7.4 %collective-permute-start.17 = (f32[4,12,36,2]{2,0,3,1:T(4,128)S(1)}, f32[4,12,36,2]{2,0,3,1:T(4,128)S(1)}, u32[]{:S(2)}, u32[]{:S(2)}) collective-permute-start(f32[4,12,36,2]{2,0,3,1:T(4,128)S(1)} %copy.39), channel_id=1, source_target_pairs={{0,1},{1,2},{2,3},{4,5},{5,6},{6,7},{8,9},{9,10},{10,11},{12,13},{... | collective-permute-start | bytes 41480 | tf_op jit(solution)/shard_map/ppermute | solution.py:20
  102.5 4.9 %collective-permute-start.16 = (f32[4,12,36,2]{2,0,3,1:T(4,128)S(1)}, f32[4,12,36,2]{2,0,3,1:T(4,128)S(1)}, u32[]{:S(2)}, u32[]{:S(2)}) collective-permute-start(f32[4,12,36,2]{2,0,3,1:T(4,128)S(1)} %copy.37), channel_id=1, source_target_pairs={{1,0},{2,1},{3,2},{5,4},{6,5},{7,6},{9,8},{10,9},{11,10},{13,12},{... | collective-permute-start | bytes 41480 | tf_op jit(solution)/shard_map/ppermute | solution.py:22
  114.1 4.4 %collective-permute-start.19 = (f32[4,2,32,128]{3,0,2,1:T(4,128)S(1)}, f32[4,2,32,128]{3,0,2,1:T(4,128)S(1)}, u32[]{:S(2)}, u32[]{:S(2)}) collective-permute-start(f32[4,2,32,128]{3,0,2,1:T(4,128)S(1)} %get-tuple-element.27), channel_id=1, source_target_pairs={{0,8},{8,16},{16,24},{1,9},{9,17},{17,25},{2,10},{10,18},{18,26},{... | collective-permute-start | bytes 393224 | tf_op jit(solution)/shard_map/ppermute | solution.py:20
  116.0 6.9 %collective-permute-start.18 = (f32[4,2,32,128]{3,0,2,1:T(4,128)S(1)}, f32[4,2,32,128]{3,0,2,1:T(4,128)S(1)}, u32[]{:S(2)}, u32[]{:S(2)}) collective-permute-start(f32[4,2,32,128]{3,0,2,1:T(4,128)S(1)} %get-tuple-element.28), channel_id=1, source_target_pairs={{8,0},{16,8},{24,16},{9,1},{17,9},{25,17},{10,2},{18,10},{26,18},{... | collective-permute-start | bytes 393224 | tf_op jit(solution)/shard_map/ppermute | solution.py:22
  122.9 3.4 %collective-permute-start.21 = (f32[4,12,2,128]{3,0,2,1:T(4,128)S(1)}, f32[4,12,2,128]{3,0,2,1:T(4,128)S(1)}, u32[]{:S(2)}, u32[]{:S(2)}) collective-permute-start(f32[4,12,2,128]{3,0,2,1:T(4,128)S(1)} %get-tuple-element.15), channel_id=1, source_target_pairs={{0,4},{1,5},{2,6},{3,7},{8,12},{9,13},{10,14},{11,15},{16,20},{17,... | collective-permute-start | bytes 147464 | tf_op jit(solution)/shard_map/ppermute | solution.py:20
  124.5 6.4 %collective-permute-start.20 = (f32[4,12,2,128]{3,0,2,1:T(4,128)S(1)}, f32[4,12,2,128]{3,0,2,1:T(4,128)S(1)}, u32[]{:S(2)}, u32[]{:S(2)}) collective-permute-start(f32[4,12,2,128]{3,0,2,1:T(4,128)S(1)} %get-tuple-element.16), channel_id=1, source_target_pairs={{4,0},{5,1},{6,2},{7,3},{12,8},{13,9},{14,10},{15,11},{20,16},{21,... | collective-permute-start | bytes 147464 | tf_op jit(solution)/shard_map/ppermute | solution.py:22
  132.5 7.4 %collective-permute-start.23 = (f32[4,12,36,2]{2,0,3,1:T(4,128)S(1)}, f32[4,12,36,2]{2,0,3,1:T(4,128)S(1)}, u32[]{:S(2)}, u32[]{:S(2)}) collective-permute-start(f32[4,12,36,2]{2,0,3,1:T(4,128)S(1)} %copy.43), channel_id=1, source_target_pairs={{0,1},{1,2},{2,3},{4,5},{5,6},{6,7},{8,9},{9,10},{10,11},{12,13},{... | collective-permute-start | bytes 41480 | tf_op jit(solution)/shard_map/ppermute | solution.py:20
  134.6 4.9 %collective-permute-start.22 = (f32[4,12,36,2]{2,0,3,1:T(4,128)S(1)}, f32[4,12,36,2]{2,0,3,1:T(4,128)S(1)}, u32[]{:S(2)}, u32[]{:S(2)}) collective-permute-start(f32[4,12,36,2]{2,0,3,1:T(4,128)S(1)} %copy.41), channel_id=1, source_target_pairs={{1,0},{2,1},{3,2},{5,4},{6,5},{7,6},{9,8},{10,9},{11,10},{13,12},{... | collective-permute-start | bytes 41480 | tf_op jit(solution)/shard_map/ppermute | solution.py:22
  148.0 20.4 %copy-start.16 = (f32[32,32]{1,0:T(8,128)S(1)}, f32[32,32]{1,0:T(8,128)}, u32[]{:S(2)}) copy-start(f32[32,32]{1,0:T(8,128)} %param.12) | copy-start | bytes 12292
  148.0 32.9 %reduce-scatter.10.cloned.1.call-start = ((), (), s32[]{:S(2)}) async-start(), calls=%async_computation.5 | async-start | bytes 49152
  170.9 34.4 %reduce-scatter.8.cloned.1.call-start = ((), (), s32[]{:S(2)}) async-start(), calls=%async_computation.4 | async-start | bytes 655360 | tf_op jit(solution)/shard_map/reduce_scatter | solution.py:79
  (19 other events, 52.5 us)
Sparse Core Ops, SparseCore 0:
  148.1 20.2 reduce-scatter.5
  171.1 9.8 reduce-scatter.9
  183.6 21.6 reduce-scatter.7
where the time goes:
time: 214 us; the launch traced here: 213 us
  waiting for transfers between devices  103 us (48%)
  starting transfers between devices  45.3 us (21%)
  matrix products  23.3 us (11%)
  local copies, waits for them, and re-layouts  22.5 us (11%)
  between operations  13.7 us (6%)
  other arithmetic  5.33 us (2%)
    ppermute x12, waiting for transfers between devices, with_halo(): lax.ppermute(head, axis, [((i + 1) % count, i) for i in range(ends)])  44.3 us
    ppermute x12, starting transfers between devices, with_halo(): lax.ppermute(tail, axis, [(i, (i + 1) % count) for i in range(ends)])  29.5 us
    reduce_scatter x1, waiting for transfers between devices, local(): lax.psum_scatter(partial_value, 'gx', scatter_dimension=1, tiled=True)  21.8 us
    dot_general x4, matrix products, tendency(): jnp.einsum('vw,wxyz->vxyz', coupling, center, precision=lax.Precision.HIG...  21.2 us
    reduce_scatter x1, waiting for transfers between devices, local(): lax.psum_scatter(partial_value, 'gz', scatter_dimension=3, tiled=True)  20.3 us
    ppermute x12, starting transfers between devices, with_halo(): lax.ppermute(head, axis, [((i + 1) % count, i) for i in range(ends)])  15.7 us
    unnamed x4, waiting for transfers between devices  9.98 us
    ppermute x12, waiting for transfers between devices, with_halo(): lax.ppermute(tail, axis, [(i, (i + 1) % count) for i in range(ends)])  6.92 us
  transfers between devices with their start and end apart: 27, of which 23 were waited for; matrix products, arithmetic and copies ran while one was open for 4% of the time, Pallas kernels for 0%

commit v1 on v0

--- a/solution.py
+++ b/solution.py
@@ -1,14 +1,20 @@
+import functools
 import jax
 import jax.numpy as jnp
 from jax import lax
+from jax.experimental import pallas as pl
+from jax.experimental.pallas import tpu as pltpu
 from jax.sharding import PartitionSpec as P
 
 STEPS = 2
+STAGES = 2 * STEPS
+HALO = 2
+PAD = 8
+MESH = pl.DeviceIdType.MESH
+HIGHEST = lax.Precision.HIGHEST
 
 
 time_step = 0.2
-
-
 def with_halo(cells, sides, width):
     for axis, dim in sides:
         count = lax.axis_size(axis)
@@ -61,7 +67,7 @@
     return with_halo(values, (("gx", 1), ("gy", 2), ("gz", 3)), 2)
 
 
-def local(fields, velocity, diffusivity, coupling, factor_x, factor_y, factor_z):
+def local_plain(fields, velocity, diffusivity, coupling, factor_x, factor_y, factor_z):
     state = fields
     for repeat in range(STEPS):
         section = state + time_step * tendency(with_edges(state), velocity, diffusivity, coupling)
@@ -80,7 +86,383 @@
     return core_tensor
 
 
+class Plan:
+    def __init__(self, mesh_shape, fields, factor_x):
+        self.nx, self.ny, self.nz = (mesh_shape[a] for a in ("gx", "gy", "gz"))
+        self.vars, self.lx, self.ly, self.lz = fields
+        self.rank = factor_x[1]
+        self.ax, self.by, self.cz = self.rank // self.nx, self.rank // self.ny, self.rank // self.nz
+        self.edge = [0, 1, self.lx - 2, self.lx - 1]
+        self.inner = list(range(2, self.lx - 2))
+        self.tiles = self.ly // 8
+
+    def fits(self):
+        return (
+            self.lz == 128
+            and self.ly % 8 == 0
+            and self.lx > 4
+            and self.lx <= 12
+            and len(self.edge) * self.tiles * 4 <= 128
+            and len(self.inner) * self.tiles * 4 <= 128
+            and self.rank % self.nx == 0 and self.rank % self.ny == 0 and self.rank % self.nz == 0
+            and self.cz % 8 == 0
+            and self.lx * self.by % 128 == 0
+            and self.ax * self.by % 128 == 0
+        )
+
+
+def kernel(
+    plan,
+    fields,
+    velocity,
+    diffusivity,
+    coupling,
+    factor_x,
+    factor_y,
+    factor_z,
+    out,
+    cells,
+    speed,
+    y_out,
+    y_in,
+    z_out,
+    z_in,
+    spread_y,
+    spread_x,
+    yz_out,
+    yz_in,
+    x_out,
+    x_in,
+    load_sem,
+    x_send,
+    x_recv,
+    ya_send,
+    ya_recv,
+    za_send,
+    za_recv,
+    yb_send,
+    yb_recv,
+    zb_send,
+    zb_recv,
+    yz_send,
+    yz_recv,
+    xs_send,
+    xs_recv,
+):
+    p = plan
+    nx, ny, nz = p.nx, p.ny, p.nz
+    lx, ly, nv = p.lx, p.ly, p.vars
+    mx, my, mz = lax.axis_index("gx"), lax.axis_index("gy"), lax.axis_index("gz")
+    rows = slice(PAD, PAD + ly)
+    low_x, high_x = mx > 0, mx < nx - 1
+    low_y, high_y = my > 0, my < ny - 1
+    low_z, high_z = mz > 0, mz < nz - 1
+
+    def remote(src, dst, send, recv, axis, to):
+        return pltpu.make_async_remote_copy(
+            src_ref=src, dst_ref=dst, send_sem=send, recv_sem=recv,
+            device_id={axis: to}, device_id_type=MESH,
+        )
+
+    def up(index, count):
+        return lax.rem(index + 1, count)
+
+    def down(index, count):
+        return lax.rem(index + count - 1, count)
+
+    def x_messages(s, v):
+        if s == 0:
+            top, bottom = fields.at[v, lx - 2:lx], fields.at[v, 0:2]
+        else:
+            top = cells.at[s, v, lx:lx + 2, rows]
+            bottom = cells.at[s, v, 2:4, rows]
+        return [
+            (high_x, low_x, remote(
+                top, cells.at[s, v, 0:2, rows],
+                x_send.at[s, v, 0], x_recv.at[s, v, 0], "gx", up(mx, nx))),
+            (low_x, high_x, remote(
+                bottom, cells.at[s, v, lx + 2:lx + 4, rows],
+                x_send.at[s, v, 1], x_recv.at[s, v, 1], "gx", down(mx, nx))),
+        ]
+
+    def yz_messages(s, group, v):
+        if group == 0:
+            ys, yr = ya_send.at[s, v], ya_recv.at[s, v]
+            zs, zr = za_send.at[s, v], za_recv.at[s, v]
+            pick = lambda ref, *lead: ref.at[(*lead, v)]
+        else:
+            ys, yr, zs, zr = yb_send.at[s], yb_recv.at[s], zb_send.at[s], zb_recv.at[s]
+            pick = lambda ref, *lead: ref.at[lead]
+        return [
+            (high_y, low_y, remote(
+                pick(y_out, s, group, 1), pick(y_in, s, group, 0),
+                ys.at[0], yr.at[0], "gy", up(my, ny))),
+            (low_y, high_y, remote(
+                pick(y_out, s, group, 0), pick(y_in, s, group, 1),
+                ys.at[1], yr.at[1], "gy", down(my, ny))),
+            (high_z, low_z, remote(
+                pick(z_out, s, group), pick(z_in, s, group, 0),
+                zs.at[0], zr.at[0], "gz", up(mz, nz))),
+            (low_z, high_z, remote(
+                pick(z_out, s, group), pick(z_in, s, group, 1),
+                zs.at[1], zr.at[1], "gz", down(mz, nz))),
+        ]
+
+    def start(messages):
+        for sends, _, copy in messages:
+            pl.when(sends)(copy.start)
+
+    def arrive(messages):
+        for _, gets, copy in messages:
+            pl.when(gets)(copy.wait_recv)
+
+    def sent(messages):
+        for sends, _, copy in messages:
+            pl.when(sends)(copy.wait_send)
+
+    lane = lax.broadcasted_iota(jnp.int32, (8, 128), 1)
+    wide = lax.broadcasted_iota(jnp.int32, (ly, 128), 1)
+    groups = (p.edge, p.inner)
+
+    def pack(s, group, v, layers):
+        z = jnp.zeros((8, 128), jnp.float32)
+        for j, value in enumerate(layers):
+            y_out[s, group, 0, v, 2 * j:2 * j + 2] = value[0:2]
+            y_out[s, group, 1, v, 2 * j:2 * j + 2] = value[ly - 2:ly]
+            for t in range(p.tiles):
+                place = 4 * (j * p.tiles + t)
+                turned = pltpu.roll(value[8 * t:8 * t + 8], (place + 2) % 128, 1)
+                z = jnp.where((lane >= place) & (lane < place + 4), turned, z)
+        z_out[s, group, v] = z
+
+    def advance(s, group, v):
+        edges = jnp.where(lane % 4 < 2, z_in[s, group, 0, v], z_in[s, group, 1, v])
+        spread = time_step * diffusivity[v]
+        rates = [time_step * coupling[v, w] for w in range(nv)]
+        keep = 1.0 - 6.0 * spread
+        layers = groups[group]
+        for j, x in enumerate(layers):
+            cells[s, v, x + 2, PAD - 2:PAD] = y_in[s, group, 0, v, 2 * j:2 * j + 2]
+            cells[s, v, x + 2, PAD + ly:PAD + ly + 2] = y_in[s, group, 1, v, 2 * j:2 * j + 2]
+        result = []
+        for j, x in enumerate(layers):
+            centre = cells[s, v, x + 2, rows]
+            beside = jnp.concatenate(
+                [pltpu.roll(edges, (126 - 4 * (j * p.tiles + t)) % 128, 1) for t in range(p.tiles)], axis=0)
+            near = [
+                (cells[s, v, x + 3, rows], cells[s, v, x + 1, rows],
+                 cells[s, v, x + 4, rows], cells[s, v, x, rows]),
+                (cells[s, v, x + 2, PAD + 1:PAD + 1 + ly], cells[s, v, x + 2, PAD - 1:PAD - 1 + ly],
+                 cells[s, v, x + 2, PAD + 2:PAD + 2 + ly], cells[s, v, x + 2, PAD - 2:PAD - 2 + ly]),
+                (pltpu.roll(jnp.where(wide == 0, beside, centre), 127, 1),
+                 pltpu.roll(jnp.where(wide == 127, beside, centre), 1, 1),
+                 pltpu.roll(jnp.where(wide <= 1, beside, centre), 126, 1),
+                 pltpu.roll(jnp.where(wide >= 126, beside, centre), 2, 1)),
+            ]
+            moved = around = None
+            for a, (next1, last1, next2, last2) in enumerate(near):
+                flow = speed[a, x] * (8.0 * (next1 - last1) - (next2 - last2))
+                both = next1 + last1
+                moved = flow if moved is None else moved + flow
+                around = both if around is None else around + both
+            factor = keep
+            for w in range(nv):
+                factor = factor + rates[w] * cells[s, w, x + 2, rows]
+            new = centre * factor + moved + spread * around
+            if s % 2 == 1:
+                new = 0.5 * (new + cells[s - 1, v, x + 2, rows])
+            cells[s + 1, v, x + 2, rows] = new
+            result.append(new)
+        return result
+
+    def clear(condition, ref, *index):
+        @pl.when(jnp.logical_not(condition))
+        def _():
+            ref[index] = jnp.zeros_like(ref[index])
+
+    for s in range(STAGES):
+        clear(low_x, cells, s, slice(None), slice(0, 2))
+        clear(high_x, cells, s, slice(None), slice(lx + 2, lx + 4))
+        for group in range(2):
+            for side, condition in ((0, low_y), (1, high_y)):
+                clear(condition, y_in, s, group, side)
+            for side, condition in ((0, low_z), (1, high_z)):
+                clear(condition, z_in, s, group, side)
+
+    load = pltpu.make_async_copy(fields, cells.at[0, :, 2:lx + 2, rows], load_sem.at[0])
+    load.start()
+    load_speed = pltpu.make_async_copy(velocity, speed, load_sem.at[1])
+    load_speed.start()
+
+    partners = [
+        {"gy": lax.rem(my + dy, ny), "gz": lax.rem(mz + dz, nz)}
+        for dy in range(ny) for dz in range(nz) if dy or dz
+    ]
+    line = [{"gx": lax.rem(mx + dx, nx)} for dx in range(1, nx)]
+    barrier = pltpu.get_barrier_semaphore()
+    for device in partners + line:
+        pl.semaphore_signal(barrier, inc=1, device_id=device, device_id_type=MESH)
+    pl.semaphore_wait(barrier, len(partners) + len(line))
+
+    for v in range(nv):
+        start(x_messages(0, v))
+    load.wait()
+
+    def first_pack(v, carry):
+        for group in range(2):
+            pack(0, group, v, [cells[0, v, x + 2, rows] for x in groups[group]])
+        start(yz_messages(0, 0, v))
+        return carry
+
+    lax.fori_loop(0, nv, first_pack, 0)
+    start(yz_messages(0, 1, None))
+    load_speed.wait()
+    speed[...] = speed[...] * (-time_step / 12.0)
+
+    chunk_y = lx * p.by
+    wide_y = ny * chunk_y
+    column = lax.broadcasted_iota(jnp.int32, (p.rank, wide_y), 1)
+    row = lax.broadcasted_iota(jnp.int32, (p.rank, wide_y), 0)
+    place_y = jnp.where(row == column // chunk_y * p.by + column % p.by, 1.0, 0.0)
+    repeated = jnp.dot(factor_y[...], place_y, precision=HIGHEST, preferred_element_type=jnp.float32)
+    column = lax.broadcasted_iota(jnp.int32, (ly, wide_y), 1)
+    for x in range(lx):
+        spread_y[x * ly:(x + 1) * ly] = jnp.where(column % chunk_y // p.by == x, repeated, 0.0)
+    chunk_x = p.ax * p.by
+    wide_x = nx * chunk_x
+    column = lax.broadcasted_iota(jnp.int32, (p.rank, wide_x), 1)
+    row = lax.broadcasted_iota(jnp.int32, (p.rank, wide_x), 0)
+    place_x = jnp.where(row == column // p.by, 1.0, 0.0)
+    repeated = jnp.dot(factor_x[...], place_x, precision=HIGHEST, preferred_element_type=jnp.float32)
+    column = lax.broadcasted_iota(jnp.int32, (p.by, wide_x), 1)
+    row = lax.broadcasted_iota(jnp.int32, (p.by, wide_x), 0)
+    for x in range(lx):
+        spread_x[x * p.by:(x + 1) * p.by] = jnp.where(column % p.by == row, repeated[x:x + 1], 0.0)
+
+    for s in range(STAGES):
+        last = s == STAGES - 1
+
+        def edge_part(v, carry):
+            messages = x_messages(s, v) + yz_messages(s, 0, v)
+            arrive(messages)
+            layers = advance(s, 0, v)
+            if not last:
+                start(x_messages(s + 1, v))
+                pack(s + 1, 0, v, layers)
+                start(yz_messages(s + 1, 0, v))
+            return carry
+
+        def inner_part(v, carry):
+            layers = advance(s, 1, v)
+            if not last:
+                pack(s + 1, 1, v, layers)
+            return carry
+
+        lax.fori_loop(0, nv, edge_part, 0)
+        arrive(yz_messages(s, 1, None))
+        lax.fori_loop(0, nv, inner_part, 0)
+        if not last:
+            start(yz_messages(s + 1, 1, None))
+
+    for v in range(nv):
+        state = cells[STAGES, v, 2:lx + 2, rows].reshape(lx * ly, p.lz)
+        reduced = lax.dot_general(
+            factor_z[...], state, (((0,), (1,)), ((), ())),
+            precision=HIGHEST, preferred_element_type=jnp.float32)
+        reduced = jnp.dot(reduced, spread_y[...], precision=HIGHEST, preferred_element_type=jnp.float32)
+        for y in range(ny):
+            for z in range(nz):
+                yz_out[y * nz + z, v] = reduced[
+                    z * p.cz:(z + 1) * p.cz, y * chunk_y:(y + 1) * chunk_y]
+    plane = []
+    for i, device in enumerate(partners):
+        plane.append(pltpu.make_async_remote_copy(
+            src_ref=yz_out.at[device["gy"] * nz + device["gz"]], dst_ref=yz_in.at[i],
+            send_sem=yz_send.at[i], recv_sem=yz_recv.at[i],
+            device_id=device, device_id_type=MESH))
+        plane[-1].start()
+    total = yz_out[my * nz + mz]
+    for i, copy in enumerate(plane):
+        copy.wait_recv()
+        total = total + yz_in[i]
+
+    total = total.reshape(nv * p.cz, chunk_y)
+    total = jnp.dot(total, spread_x[...], precision=HIGHEST, preferred_element_type=jnp.float32)
+    for x in range(nx):
+        x_out[x] = total[:, x * chunk_x:(x + 1) * chunk_x].reshape(nv, p.cz, chunk_x)
+    along = []
+    for i, device in enumerate(line):
+        along.append(pltpu.make_async_remote_copy(
+            src_ref=x_out.at[device["gx"]], dst_ref=x_in.at[i],
+            send_sem=xs_send.at[i], recv_sem=xs_recv.at[i],
+            device_id=device, device_id_type=MESH))
+        along[-1].start()
+    total = x_out[mx]
+    for i, copy in enumerate(along):
+        copy.wait_recv()
+        total = total + x_in[i]
+    out[...] = total
+
+    for s in range(STAGES):
+        def edge_sent(v, carry):
+            sent(x_messages(s, v) + yz_messages(s, 0, v))
+            return carry
+
+        lax.fori_loop(0, nv, edge_sent, 0)
+        sent(yz_messages(s, 1, None))
+    for copy in plane + along:
+        copy.wait_send()
+
+
+def local_kernel(plan, fields, velocity, diffusivity, coupling, factor_x, factor_y, factor_z):
+    p = plan
+    nv, lx, ly = p.vars, p.lx, p.ly
+    chunk_y, chunk_x = lx * p.by, p.ax * p.by
+    others = p.ny * p.nz - 1
+    vmem = lambda *shape: pltpu.VMEM(shape, jnp.float32)
+    dma = lambda *shape: pltpu.SemaphoreType.DMA(shape)
+    whole = pl.BlockSpec(memory_space=pltpu.VMEM)
+    scalars = pl.BlockSpec(memory_space=pltpu.SMEM)
+    result = pl.pallas_call(
+        functools.partial(kernel, p),
+        out_shape=jax.ShapeDtypeStruct((nv, p.cz, chunk_x), jnp.float32),
+        in_specs=[pl.BlockSpec(memory_space=pl.ANY)] * 2 + [scalars] * 2 + [whole] * 3,
+        out_specs=whole,
+        scratch_shapes=[
+            vmem(STAGES + 1, nv, lx + 4, ly + 2 * PAD, p.lz),
+            vmem(3, lx, ly, p.lz),
+            vmem(STAGES, 2, 2, nv, 8 * -(-max(4, lx - 4) // 4), p.lz),
+            vmem(STAGES, 2, 2, nv, 8 * -(-max(4, lx - 4) // 4), p.lz),
+            vmem(STAGES, 2, nv, 8, 128),
+            vmem(STAGES, 2, 2, nv, 8, 128),
+            vmem(lx * ly, p.ny * chunk_y),
+            vmem(chunk_y, p.nx * chunk_x),
+            vmem(p.ny * p.nz, nv, p.cz, chunk_y),
+            vmem(others, nv, p.cz, chunk_y),
+            vmem(p.nx, nv, p.cz, chunk_x),
+            vmem(p.nx - 1, nv, p.cz, chunk_x),
+            dma(2),
+            dma(STAGES, nv, 2), dma(STAGES, nv, 2),
+            dma(STAGES, nv, 2), dma(STAGES, nv, 2),
+            dma(STAGES, nv, 2), dma(STAGES, nv, 2),
+            dma(STAGES, 2), dma(STAGES, 2),
+            dma(STAGES, 2), dma(STAGES, 2),
+            dma(others), dma(others),
+            dma(p.nx - 1), dma(p.nx - 1),
+        ],
+        compiler_params=pltpu.CompilerParams(
+            collective_id=0, has_side_effects=True, vmem_limit_bytes=40 * 1024 * 1024),
+    )(fields, velocity, diffusivity, coupling, factor_x, factor_y, factor_z)
+    result = result.reshape(nv, p.cz, p.ax, p.by)
+    return jnp.transpose(result, (0, 2, 3, 1))
+
+
 def solution(mesh):
+    def local(fields, velocity, diffusivity, coupling, factor_x, factor_y, factor_z):
+        plan = Plan(mesh.shape, fields.shape, factor_x.shape)
+        run = functools.partial(local_kernel, plan) if plan.fits() else local_plain
+        return run(fields, velocity, diffusivity, coupling, factor_x, factor_y, factor_z)
+
     return jax.shard_map(
         local,
         mesh=mesh,

time: 214 us -> 39 us (0.18)
  waiting for transfers between devices: 103 us -> 0 us
  starting transfers between devices: 45.3 us -> 0 us
  Pallas kernels: 0 us -> 35 us
  matrix products: 23.3 us -> 0 us
  local copies, waits for them, and re-layouts: 22.5 us -> 3.69 us
  between operations: 13.7 us -> 0.06 us
  other arithmetic: 5.33 us -> 0 us
    ppermute x24 -> x0, waiting for transfers between devices: 51.2 us -> none  [the longest x12 44.3 us: with_halo(): lax.ppermute(head, axis, [((i + 1) % count, i) for i in range(ends)])]
    ppermute x24 -> x0, starting transfers between devices: 45.2 us -> none  [the longest x12 29.5 us: with_halo(): lax.ppermute(tail, axis, [(i, (i + 1) % count) for i in range(ends)])]
    reduce_scatter x2 -> x0, waiting for transfers between devices: 42.1 us -> none  [the longest x1 21.8 us: local(): lax.psum_scatter(partial_value, 'gx', scatter_dimension=1, tiled=True)]
    pallas_call x0 -> x1, Pallas kernels: none -> 35 us  [local_kernel(): pl.pallas_call(functools.partial(kernel, p), out_shape=jax.ShapeDtypeStru...]
    dot_general x7 -> x0, matrix products: 23.3 us -> none  [the longest x4 21.2 us: tendency(): jnp.einsum('vw,wxyz->vxyz', coupling, center, precision=lax.Precision.HIG...]
    unnamed x4 -> x0, waiting for transfers between devices: 9.98 us -> none
    slice x17 -> x0, local copies, waits for them, and re-layouts: 6.65 us -> none  [the longest x9 4.82 us: with_halo(): head = lax.slice_in_dim(cells, 0, width, axis=dim)]
    ppermute x8 -> x0, local copies, waits for them, and re-layouts: 6.61 us -> none  [the longest x4 3.8 us: with_halo(): lax.ppermute(tail, axis, [(i, (i + 1) % count) for i in range(ends)])]
  transfers between devices with their start and end apart: 27 -> 0, of which waited for: 23 -> 0; matrix products, arithmetic and copies ran while one was open for 4% -> 0% of each run, Pallas kernels for 0% -> 0%
where the time goes in v1:
time: 39 us; the launch traced here: 38.8 us
  Pallas kernels  35 us (90%)
  local copies, waits for them, and re-layouts  3.69 us (9%)
    pallas_call x1, Pallas kernels, local_kernel(): pl.pallas_call(functools.partial(kernel, p), out_shape=jax.ShapeDtypeStru...  35 us
    unnamed x13, local copies, waits for them, and re-layouts  2.91 us

profile of v1, /device:TPU:0, one launch (start us, length us, event | category | flops | bytes accessed | tf_op | source)
XLA Modules:
  0.0 38.8 jit_solution(15189361466239172828)
XLA Ops:
  0.0 0.0 copy-start.2
  0.0 0.0 copy-start.3
  0.0 0.0 copy-start.4
  0.0 0.0 copy-start.5
  0.0 0.9 %copy.8.factor_z = f32[128,32]{1,0:T(8,128)S(1)} copy(f32[128,32]{0,1:T(8,128)} %param.13) | data formatting | bytes 32768 | tf_op args[6]
  0.9 0.0 copy-done.2
  0.9 0.0 copy-done.3
  0.9 0.0 copy-done.4
  0.9 0.0 copy-done.5
  0.9 0.0 copy-start
  0.9 1.0 %copy-done = f32[4,8,32,128]{3,2,1,0:T(8,128)S(1)} copy-done((f32[4,8,32,128]{3,2,1,0:T(8,128)S(1)}, f32[4,8,32,128]{3,2,1,0:T(8,128)}, u32[]{:S(2)}) %copy-start) | copy-done | bytes 524312
  2.0 0.0 copy-start.1
  2.0 1.0 %copy-done.1 = f32[3,8,32,128]{3,2,1,0:T(8,128)S(1)} copy-done((f32[3,8,32,128]{3,2,1,0:T(8,128)S(1)}, f32[3,8,32,128]{3,2,1,0:T(8,128)}, u32[]{:S(2)}) %copy-start.1) | copy-done | bytes 393240
  3.0 35.0 %shard_map.73 = f32[4,8,128]{2,1,0:T(8,128)S(1)} custom-call(f32[4,8,32,128]{3,2,1,0:T(8,128)S(1)} %copy-done, f32[3,8,32,128]{3,2,1,0:T(8,128)S(1)} %copy-done.1, f32[4]{0:T(128)S(1)} %copy-done.5, f32[4,4]{1,0:T(4,128)S(1)} %copy-done.4, f32[8,32]{1,0:T(8,128)S(1)} %copy-done.3, f32[32,32]{1,0:T(8,128)S(1)} %copy-done.2, f32[128,32]{1,0:T(8,128)S(1)} %copy.8.factor_z), custom_call_target="tpu_custom_call" | custom-call | tf_op jit(solution)/shard_map/pallas_call | solution.py:426
  38.0 0.1 reshape.3
  38.1 0.7 %copy.11 = f32[4,8,8,16]{3,1,2,0:T(8,128)} copy(f32[4,8,8,16]{3,2,1,0:T(8,128)S(1)} %reshape.3) | data formatting | bytes 32768 | tf_op jit(solution)/shard_map/reshape | solution.py:456
Async XLA Ops:
  0.0 0.9 %copy-start.2 = (f32[32,32]{1,0:T(8,128)S(1)}, f32[32,32]{1,0:T(8,128)}, u32[]{:S(2)}) copy-start(f32[32,32]{1,0:T(8,128)} %factor_y.1) | copy-start | bytes 12292
  0.0 0.9 %copy-start.3 = (f32[8,32]{1,0:T(8,128)S(1)}, f32[8,32]{1,0:T(8,128)}, u32[]{:S(2)}) copy-start(f32[8,32]{1,0:T(8,128)} %factor_x.1) | copy-start | bytes 3076
  0.0 0.9 %copy-start.4 = (f32[4,4]{1,0:T(4,128)S(1)}, f32[4,4]{1,0:T(4,128)}, u32[]{:S(2)}) copy-start(f32[4,4]{1,0:T(4,128)} %coupling.1) | copy-start | bytes 196
  0.0 0.9 %copy-start.5 = (f32[4]{0:T(128)S(1)}, f32[4]{0:T(128)}, u32[]{:S(2)}) copy-start(f32[4]{0:T(128)} %diffusivity.1) | copy-start | bytes 52
  0.9 1.0 %copy-start = (f32[4,8,32,128]{3,2,1,0:T(8,128)S(1)}, f32[4,8,32,128]{3,2,1,0:T(8,128)}, u32[]{:S(2)}) copy-start(f32[4,8,32,128]{3,2,1,0:T(8,128)} %fields.1) | copy-start | bytes 1572868
  2.0 1.0 %copy-start.1 = (f32[3,8,32,128]{3,2,1,0:T(8,128)S(1)}, f32[3,8,32,128]{3,2,1,0:T(8,128)}, u32[]{:S(2)}) copy-start(f32[3,8,32,128]{3,2,1,0:T(8,128)} %velocity.1) | copy-start | bytes 1179652

commit v2 on v1

--- a/solution.py
+++ b/solution.py
@@ -9,6 +9,7 @@
 STEPS = 2
 STAGES = 2 * STEPS
 HALO = 2
+PAIR = 2
 PAD = 8
 MESH = pl.DeviceIdType.MESH
 HIGHEST = lax.Precision.HIGHEST
@@ -100,6 +101,8 @@
         return (
             self.lz == 128
             and self.ly % 8 == 0
+            and min(self.nx, self.ny, self.nz) > 1
+            and self.vars % PAIR == 0
             and self.lx > 4
             and self.lx <= 12
             and len(self.edge) * self.tiles * 4 <= 128
@@ -136,14 +139,10 @@
     load_sem,
     x_send,
     x_recv,
-    ya_send,
-    ya_recv,
-    za_send,
-    za_recv,
-    yb_send,
-    yb_recv,
-    zb_send,
-    zb_recv,
+    y_send,
+    y_recv,
+    z_send,
+    z_recv,
     yz_send,
     yz_recv,
     xs_send,
@@ -179,49 +178,79 @@
         return [
             (high_x, low_x, remote(
                 top, cells.at[s, v, 0:2, rows],
-                x_send.at[s, v, 0], x_recv.at[s, v, 0], "gx", up(mx, nx))),
+                x_send.at[0], x_recv.at[s, v, 0], "gx", up(mx, nx))),
             (low_x, high_x, remote(
                 bottom, cells.at[s, v, lx + 2:lx + 4, rows],
-                x_send.at[s, v, 1], x_recv.at[s, v, 1], "gx", down(mx, nx))),
+                x_send.at[1], x_recv.at[s, v, 1], "gx", down(mx, nx))),
         ]
 
-    def yz_messages(s, group, v):
+    chunks = nv // PAIR
+
+    def yz_messages(s, group, c):
         if group == 0:
-            ys, yr = ya_send.at[s, v], ya_recv.at[s, v]
-            zs, zr = za_send.at[s, v], za_recv.at[s, v]
-            pick = lambda ref, *lead: ref.at[(*lead, v)]
-        else:
-            ys, yr, zs, zr = yb_send.at[s], yb_recv.at[s], zb_send.at[s], zb_recv.at[s]
-            pick = lambda ref, *lead: ref.at[lead]
-        return [
-            (high_y, low_y, remote(
-                pick(y_out, s, group, 1), pick(y_in, s, group, 0),
-                ys.at[0], yr.at[0], "gy", up(my, ny))),
-            (low_y, high_y, remote(
-                pick(y_out, s, group, 0), pick(y_in, s, group, 1),
-                ys.at[1], yr.at[1], "gy", down(my, ny))),
-            (high_z, low_z, remote(
-                pick(z_out, s, group), pick(z_in, s, group, 0),
-                zs.at[0], zr.at[0], "gz", up(mz, nz))),
-            (low_z, high_z, remote(
-                pick(z_out, s, group), pick(z_in, s, group, 1),
-                zs.at[1], zr.at[1], "gz", down(mz, nz))),
+            which, place = pl.ds(c * PAIR, PAIR), c
+        else:
+            which, place = slice(None), chunks
+        result = [
+            (None, None, remote(
+                z_out.at[s, group, which], z_in.at[s, group, 0, which],
+                z_send.at[0], z_recv.at[s, place, 0], "gz", up(mz, nz))),
+            (None, None, remote(
+                z_out.at[s, group, which], z_in.at[s, group, 1, which],
+                z_send.at[1], z_recv.at[s, place, 1], "gz", down(mz, nz))),
         ]
+        if ny == 2:
+            result.append((None, None, remote(
+                y_out.at[s, group, 1 - my, which], y_in.at[s, group, my, which],
+                y_send.at[0], y_recv.at[s, place, 0], "gy", 1 - my)))
+        else:
+            result += [
+                (high_y, low_y, remote(
+                    y_out.at[s, group, 1, which], y_in.at[s, group, 0, which],
+                    y_send.at[0], y_recv.at[s, place, 0], "gy", up(my, ny))),
+                (low_y, high_y, remote(
+                    y_out.at[s, group, 0, which], y_in.at[s, group, 1, which],
+                    y_send.at[1], y_recv.at[s, place, 1], "gy", down(my, ny))),
+            ]
+        return result
+
+    def guarded(condition, action):
+        if condition is None:
+            action()
+        else:
+            pl.when(condition)(action)
 
     def start(messages):
         for sends, _, copy in messages:
-            pl.when(sends)(copy.start)
+            guarded(sends, copy.start)
 
     def arrive(messages):
         for _, gets, copy in messages:
-            pl.when(gets)(copy.wait_recv)
-
-    def sent(messages):
-        for sends, _, copy in messages:
-            pl.when(sends)(copy.wait_send)
+            guarded(gets, copy.wait_recv)
+
+    def all_sent():
+        layers = cells.at[0:STAGES, :, 0:2, rows]
+        waits = [
+            (high_x, remote(layers, layers, x_send.at[0], x_recv.at[0, 0, 0], "gx", up(mx, nx))),
+            (low_x, remote(layers, layers, x_send.at[1], x_recv.at[0, 0, 1], "gx", down(mx, nx))),
+            (None, remote(z_out, z_out, z_send.at[0], z_recv.at[0, 0, 0], "gz", up(mz, nz))),
+            (None, remote(z_out, z_out, z_send.at[1], z_recv.at[0, 0, 1], "gz", down(mz, nz))),
+        ]
+        half = y_out.at[:, :, 0]
+        if ny == 2:
+            waits.append((None, remote(half, half, y_send.at[0], y_recv.at[0, 0, 0], "gy", 1 - my)))
+        else:
+            waits += [
+                (high_y, remote(half, half, y_send.at[0], y_recv.at[0, 0, 0], "gy", up(my, ny))),
+                (low_y, remote(half, half, y_send.at[1], y_recv.at[0, 0, 1], "gy", down(my, ny))),
+            ]
+        for condition, copy in waits:
+            guarded(condition, copy.wait_send)
 
     lane = lax.broadcasted_iota(jnp.int32, (8, 128), 1)
-    wide = lax.broadcasted_iota(jnp.int32, (ly, 128), 1)
+    quarter = lax.shift_right_logical(lane, 2)
+    lower = jnp.bitwise_and(lane, 3) < 2
+    inside = jnp.where(lower, jnp.minimum(mz, 1), jnp.minimum(nz - 1 - mz, 1)) > 0
     groups = (p.edge, p.inner)
 
     def pack(s, group, v, layers):
@@ -232,11 +261,12 @@
             for t in range(p.tiles):
                 place = 4 * (j * p.tiles + t)
                 turned = pltpu.roll(value[8 * t:8 * t + 8], (place + 2) % 128, 1)
-                z = jnp.where((lane >= place) & (lane < place + 4), turned, z)
+                z = jnp.where(quarter == j * p.tiles + t, turned, z)
         z_out[s, group, v] = z
 
     def advance(s, group, v):
-        edges = jnp.where(lane % 4 < 2, z_in[s, group, 0, v], z_in[s, group, 1, v])
+        edges = jnp.where(lower, z_in[s, group, 0, v], z_in[s, group, 1, v])
+        edges = jnp.where(inside, edges, 0.0)
         spread = time_step * diffusivity[v]
         rates = [time_step * coupling[v, w] for w in range(nv)]
         keep = 1.0 - 6.0 * spread
@@ -247,17 +277,19 @@
         result = []
         for j, x in enumerate(layers):
             centre = cells[s, v, x + 2, rows]
-            beside = jnp.concatenate(
-                [pltpu.roll(edges, (126 - 4 * (j * p.tiles + t)) % 128, 1) for t in range(p.tiles)], axis=0)
+            turned = [[], [], [], []]
+            for t in range(p.tiles):
+                tile = centre[8 * t:8 * t + 8]
+                beside = pltpu.roll(edges, (126 - 4 * (j * p.tiles + t)) % 128, 1)
+                for i, (mask, shift) in enumerate(
+                        ((lane == 0, 127), (lane == 127, 1), (lane <= 1, 126), (lane >= 126, 2))):
+                    turned[i].append(pltpu.roll(jnp.where(mask, beside, tile), shift, 1))
             near = [
                 (cells[s, v, x + 3, rows], cells[s, v, x + 1, rows],
                  cells[s, v, x + 4, rows], cells[s, v, x, rows]),
                 (cells[s, v, x + 2, PAD + 1:PAD + 1 + ly], cells[s, v, x + 2, PAD - 1:PAD - 1 + ly],
                  cells[s, v, x + 2, PAD + 2:PAD + 2 + ly], cells[s, v, x + 2, PAD - 2:PAD - 2 + ly]),
-                (pltpu.roll(jnp.where(wide == 0, beside, centre), 127, 1),
-                 pltpu.roll(jnp.where(wide == 127, beside, centre), 1, 1),
-                 pltpu.roll(jnp.where(wide <= 1, beside, centre), 126, 1),
-                 pltpu.roll(jnp.where(wide >= 126, beside, centre), 2, 1)),
+                tuple(jnp.concatenate(parts, axis=0) for parts in turned),
             ]
             moved = around = None
             for a, (next1, last1, next2, last2) in enumerate(near):
@@ -286,8 +318,6 @@
         for group in range(2):
             for side, condition in ((0, low_y), (1, high_y)):
                 clear(condition, y_in, s, group, side)
-            for side, condition in ((0, low_z), (1, high_z)):
-                clear(condition, z_in, s, group, side)
 
     load = pltpu.make_async_copy(fields, cells.at[0, :, 2:lx + 2, rows], load_sem.at[0])
     load.start()
@@ -308,16 +338,27 @@
         start(x_messages(0, v))
     load.wait()
 
-    def first_pack(v, carry):
-        for group in range(2):
-            pack(0, group, v, [cells[0, v, x + 2, rows] for x in groups[group]])
-        start(yz_messages(0, 0, v))
+    def first_pack(c, carry):
+        for v in (c * PAIR + i for i in range(PAIR)):
+            for group in range(2):
+                pack(0, group, v, [cells[0, v, x + 2, rows] for x in groups[group]])
+        start(yz_messages(0, 0, c))
         return carry
 
-    lax.fori_loop(0, nv, first_pack, 0)
+    lax.fori_loop(0, chunks, first_pack, 0)
     start(yz_messages(0, 1, None))
     load_speed.wait()
     speed[...] = speed[...] * (-time_step / 12.0)
+
+    def split(value):
+        high = value.astype(jnp.bfloat16)
+        return high, (value - high.astype(jnp.float32)).astype(jnp.bfloat16)
+
+    def product(a, b, contract=((1,), (0,))):
+        (a_high, a_low), (b_high, b_low) = a, b
+        dot = functools.partial(
+            lax.dot_general, dimension_numbers=(contract, ((), ())), preferred_element_type=jnp.float32)
+        return dot(a_high, b_high) + (dot(a_high, b_low) + dot(a_low, b_high))
 
     chunk_y = lx * p.by
     wide_y = ny * chunk_y
@@ -325,31 +366,48 @@
     row = lax.broadcasted_iota(jnp.int32, (p.rank, wide_y), 0)
     place_y = jnp.where(row == column // chunk_y * p.by + column % p.by, 1.0, 0.0)
     repeated = jnp.dot(factor_y[...], place_y, precision=HIGHEST, preferred_element_type=jnp.float32)
-    column = lax.broadcasted_iota(jnp.int32, (ly, wide_y), 1)
+    column = lax.broadcasted_iota(jnp.int32, (ly, wide_y), 1) % chunk_y // p.by
     for x in range(lx):
-        spread_y[x * ly:(x + 1) * ly] = jnp.where(column % chunk_y // p.by == x, repeated, 0.0)
+        for i, part in enumerate(split(jnp.where(column == x, repeated, 0.0))):
+            spread_y[i, x * ly:(x + 1) * ly] = part
     chunk_x = p.ax * p.by
     wide_x = nx * chunk_x
     column = lax.broadcasted_iota(jnp.int32, (p.rank, wide_x), 1)
     row = lax.broadcasted_iota(jnp.int32, (p.rank, wide_x), 0)
     place_x = jnp.where(row == column // p.by, 1.0, 0.0)
     repeated = jnp.dot(factor_x[...], place_x, precision=HIGHEST, preferred_element_type=jnp.float32)
-    column = lax.broadcasted_iota(jnp.int32, (p.by, wide_x), 1)
+    column = lax.broadcasted_iota(jnp.int32, (p.by, wide_x), 1) % p.by
     row = lax.broadcasted_iota(jnp.int32, (p.by, wide_x), 0)
     for x in range(lx):
-        spread_x[x * p.by:(x + 1) * p.by] = jnp.where(column % p.by == row, repeated[x:x + 1], 0.0)
+        for i, part in enumerate(split(jnp.where(column == row, repeated[x:x + 1], 0.0))):
+            spread_x[i, x * p.by:(x + 1) * p.by] = part
 
     for s in range(STAGES):
         last = s == STAGES - 1
 
-        def edge_part(v, carry):
-            messages = x_messages(s, v) + yz_messages(s, 0, v)
-            arrive(messages)
-            layers = advance(s, 0, v)
+        def project(v):
+            state = cells[STAGES, v, 2:lx + 2, rows].reshape(lx * ly, p.lz)
+            reduced = product(split(factor_z[...]), split(state), ((1,), (1,)))
+            reduced = product(split(reduced), (spread_y[0], spread_y[1]))
+            for y in range(ny):
+                for z in range(nz):
+                    yz_out[y * nz + z, v] = reduced[
+                        z * p.cz:(z + 1) * p.cz, y * chunk_y:(y + 1) * chunk_y]
+
+        def edge_part(c, carry):
+            for i in range(PAIR):
+                v = c * PAIR + i
+                if i == 0:
+                    arrive(yz_messages(s, 0, c))
+                arrive(x_messages(s, v))
+                layers = advance(s, 0, v)
+                if last:
+                    project(v)
+                else:
+                    start(x_messages(s + 1, v))
+                    pack(s + 1, 0, v, layers)
             if not last:
-                start(x_messages(s + 1, v))
-                pack(s + 1, 0, v, layers)
-                start(yz_messages(s + 1, 0, v))
+                start(yz_messages(s + 1, 0, c))
             return carry
 
         def inner_part(v, carry):
@@ -358,22 +416,15 @@
                 pack(s + 1, 1, v, layers)
             return carry
 
-        lax.fori_loop(0, nv, edge_part, 0)
+        if not last:
+            lax.fori_loop(0, chunks, edge_part, 0)
         arrive(yz_messages(s, 1, None))
         lax.fori_loop(0, nv, inner_part, 0)
         if not last:
             start(yz_messages(s + 1, 1, None))
-
-    for v in range(nv):
-        state = cells[STAGES, v, 2:lx + 2, rows].reshape(lx * ly, p.lz)
-        reduced = lax.dot_general(
-            factor_z[...], state, (((0,), (1,)), ((), ())),
-            precision=HIGHEST, preferred_element_type=jnp.float32)
-        reduced = jnp.dot(reduced, spread_y[...], precision=HIGHEST, preferred_element_type=jnp.float32)
-        for y in range(ny):
-            for z in range(nz):
-                yz_out[y * nz + z, v] = reduced[
-                    z * p.cz:(z + 1) * p.cz, y * chunk_y:(y + 1) * chunk_y]
+        else:
+            lax.fori_loop(0, chunks, edge_part, 0)
+
     plane = []
     for i, device in enumerate(partners):
         plane.append(pltpu.make_async_remote_copy(
@@ -387,7 +438,7 @@
         total = total + yz_in[i]
 
     total = total.reshape(nv * p.cz, chunk_y)
-    total = jnp.dot(total, spread_x[...], precision=HIGHEST, preferred_element_type=jnp.float32)
+    total = product(split(total), (spread_x[0], spread_x[1]))
     for x in range(nx):
         x_out[x] = total[:, x * chunk_x:(x + 1) * chunk_x].reshape(nv, p.cz, chunk_x)
     along = []
@@ -403,13 +454,7 @@
         total = total + x_in[i]
     out[...] = total
 
-    for s in range(STAGES):
-        def edge_sent(v, carry):
-            sent(x_messages(s, v) + yz_messages(s, 0, v))
-            return carry
-
-        lax.fori_loop(0, nv, edge_sent, 0)
-        sent(yz_messages(s, 1, None))
+    all_sent()
     for copy in plane + along:
         copy.wait_send()
 
@@ -426,7 +471,7 @@
     result = pl.pallas_call(
         functools.partial(kernel, p),
         out_shape=jax.ShapeDtypeStruct((nv, p.cz, chunk_x), jnp.float32),
-        in_specs=[pl.BlockSpec(memory_space=pl.ANY)] * 2 + [scalars] * 2 + [whole] * 3,
+        in_specs=[pl.BlockSpec(memory_space=pltpu.HBM)] * 2 + [scalars] * 2 + [whole] * 3,
         out_specs=whole,
         scratch_shapes=[
             vmem(STAGES + 1, nv, lx + 4, ly + 2 * PAD, p.lz),
@@ -435,24 +480,22 @@
             vmem(STAGES, 2, 2, nv, 8 * -(-max(4, lx - 4) // 4), p.lz),
             vmem(STAGES, 2, nv, 8, 128),
             vmem(STAGES, 2, 2, nv, 8, 128),
-            vmem(lx * ly, p.ny * chunk_y),
-            vmem(chunk_y, p.nx * chunk_x),
+            pltpu.VMEM((2, lx * ly, p.ny * chunk_y), jnp.bfloat16),
+            pltpu.VMEM((2, chunk_y, p.nx * chunk_x), jnp.bfloat16),
             vmem(p.ny * p.nz, nv, p.cz, chunk_y),
             vmem(others, nv, p.cz, chunk_y),
             vmem(p.nx, nv, p.cz, chunk_x),
             vmem(p.nx - 1, nv, p.cz, chunk_x),
             dma(2),
-            dma(STAGES, nv, 2), dma(STAGES, nv, 2),
-            dma(STAGES, nv, 2), dma(STAGES, nv, 2),
-            dma(STAGES, nv, 2), dma(STAGES, nv, 2),
-            dma(STAGES, 2), dma(STAGES, 2),
-            dma(STAGES, 2), dma(STAGES, 2),
+            dma(2), dma(STAGES, nv, 2),
+            dma(2), dma(STAGES, nv // PAIR + 1, 2),
+            dma(2), dma(STAGES, nv // PAIR + 1, 2),
             dma(others), dma(others),
             dma(p.nx - 1), dma(p.nx - 1),
         ],
         compiler_params=pltpu.CompilerParams(
             collective_id=0, has_side_effects=True, vmem_limit_bytes=40 * 1024 * 1024),
-    )(fields, velocity, diffusivity, coupling, factor_x, factor_y, factor_z)
+    )(fields, velocity, diffusivity, coupling, factor_x, factor_y, factor_z.T)
     result = result.reshape(nv, p.cz, p.ax, p.by)
     return jnp.transpose(result, (0, 2, 3, 1))
 

time: 39 us -> 41.2 us (1.056)
  local copies, waits for them, and re-layouts: 3.69 us -> 6.26 us
  Pallas kernels: 35 us -> 34.5 us
    unnamed x13 -> x14, local copies, waits for them, and re-layouts: 2.91 us -> 5.49 us
    pallas_call x1, Pallas kernels: 35 us -> 34.5 us  [local_kernel(): pl.pallas_call(functools.partial(kernel, p), out_shape=jax.ShapeDtypeStru...]
where the time goes in v2:
time: 41.2 us; the launch traced here: 40.8 us
  Pallas kernels  34.5 us (84%)
  local copies, waits for them, and re-layouts  6.26 us (15%)
    pallas_call x1, Pallas kernels, local_kernel(): pl.pallas_call(functools.partial(kernel, p), out_shape=jax.ShapeDtypeStru...  34.5 us
    unnamed x14, local copies, waits for them, and re-layouts  5.49 us

profile of v2, /device:TPU:0, one launch (start us, length us, event | category | flops | bytes accessed | tf_op | source)
XLA Modules:
  0.0 40.8 jit_solution(4652835112255096821)
XLA Ops:
  0.0 0.0 copy-start.6
  0.0 0.7 %copy-done.6 = f32[4]{0:T(128)S(1)} copy-done((f32[4]{0:T(128)S(1)}, f32[4]{0:T(128)}, u32[]{:S(2)}) %copy-start.6) | copy-done | bytes 40
  0.7 0.0 copy-start
  0.7 1.0 %copy-done = f32[4,8,32,128]{3,2,1,0:T(8,128)S(1)} copy-done((f32[4,8,32,128]{3,2,1,0:T(8,128)S(1)}, f32[4,8,32,128]{3,2,1,0:T(8,128)}, u32[]{:S(2)}) %copy-start) | copy-done | bytes 524312
  1.7 0.0 copy-start.1
  1.7 1.0 %copy-done.1 = f32[3,8,32,128]{3,2,1,0:T(8,128)S(1)} copy-done((f32[3,8,32,128]{3,2,1,0:T(8,128)S(1)}, f32[3,8,32,128]{3,2,1,0:T(8,128)}, u32[]{:S(2)}) %copy-start.1) | copy-done | bytes 393240
  2.7 0.0 copy-start.2
  2.7 0.7 %copy-done.2 = f32[32,32]{1,0:T(8,128)S(1)} copy-done((f32[32,32]{1,0:T(8,128)S(1)}, f32[32,32]{1,0:T(8,128)}, u32[]{:S(2)}) %copy-start.2) | copy-done | bytes 4120
  3.4 0.0 copy-start.3
  3.4 0.7 %copy-done.3 = f32[128,32]{0,1:T(8,128)S(1)} copy-done((f32[128,32]{0,1:T(8,128)S(1)}, f32[128,32]{0,1:T(8,128)}, u32[]{:S(2)}) %copy-start.3) | copy-done | bytes 16408
  4.1 0.0 copy-start.4
  4.1 0.7 %copy-done.4 = f32[8,32]{1,0:T(8,128)S(1)} copy-done((f32[8,32]{1,0:T(8,128)S(1)}, f32[8,32]{1,0:T(8,128)}, u32[]{:S(2)}) %copy-start.4) | copy-done | bytes 1048
  4.8 0.0 copy-start.5
  4.8 0.7 %copy-done.5 = f32[4,4]{1,0:T(4,128)S(1)} copy-done((f32[4,4]{1,0:T(4,128)S(1)}, f32[4,4]{1,0:T(4,128)}, u32[]{:S(2)}) %copy-start.5) | copy-done | bytes 88
  5.5 34.5 %shard_map.73 = f32[4,8,128]{2,1,0:T(8,128)S(1)} custom-call(f32[4,8,32,128]{3,2,1,0:T(8,128)S(1)} %copy-done, f32[3,8,32,128]{3,2,1,0:T(8,128)S(1)} %copy-done.1, f32[4]{0:T(128)S(1)} %copy-done.6, f32[4,4]{1,0:T(4,128)S(1)} %copy-done.5, f32[8,32]{1,0:T(8,128)S(1)} %copy-done.4, f32[32,32]{1,0:T(8,128)S(1)} %copy-done.2, f32[32,128]{1,0:T(8,128)S(1)} %bitcast.4), custom_call_target="tpu_custom_call" | custom-call | tf_op jit(solution)/shard_map/pallas_call | solution.py:471
  40.0 0.1 reshape.3
  40.1 0.7 %copy.10 = f32[4,8,8,16]{3,1,2,0:T(8,128)} copy(f32[4,8,8,16]{3,2,1,0:T(8,128)S(1)} %reshape.3) | data formatting | bytes 32768 | tf_op jit(solution)/shard_map/reshape | solution.py:499
Async XLA Ops:
  0.0 0.7 %copy-start.6 = (f32[4]{0:T(128)S(1)}, f32[4]{0:T(128)}, u32[]{:S(2)}) copy-start(f32[4]{0:T(128)} %diffusivity.1) | copy-start | bytes 52
  0.7 1.0 %copy-start = (f32[4,8,32,128]{3,2,1,0:T(8,128)S(1)}, f32[4,8,32,128]{3,2,1,0:T(8,128)}, u32[]{:S(2)}) copy-start(f32[4,8,32,128]{3,2,1,0:T(8,128)} %fields.1) | copy-start | bytes 1572868
  1.7 1.0 %copy-start.1 = (f32[3,8,32,128]{3,2,1,0:T(8,128)S(1)}, f32[3,8,32,128]{3,2,1,0:T(8,128)}, u32[]{:S(2)}) copy-start(f32[3,8,32,128]{3,2,1,0:T(8,128)} %velocity.1) | copy-start | bytes 1179652
  2.7 0.7 %copy-start.2 = (f32[32,32]{1,0:T(8,128)S(1)}, f32[32,32]{1,0:T(8,128)}, u32[]{:S(2)}) copy-start(f32[32,32]{1,0:T(8,128)} %factor_y.1) | copy-start | bytes 12292
  3.4 0.7 %copy-start.3 = (f32[128,32]{0,1:T(8,128)S(1)}, f32[128,32]{0,1:T(8,128)}, u32[]{:S(2)}) copy-start(f32[128,32]{0,1:T(8,128)} %param.13) | copy-start | bytes 49156
  4.1 0.7 %copy-start.4 = (f32[8,32]{1,0:T(8,128)S(1)}, f32[8,32]{1,0:T(8,128)}, u32[]{:S(2)}) copy-start(f32[8,32]{1,0:T(8,128)} %factor_x.1) | copy-start | bytes 3076
  4.8 0.7 %copy-start.5 = (f32[4,4]{1,0:T(4,128)S(1)}, f32[4,4]{1,0:T(4,128)}, u32[]{:S(2)}) copy-start(f32[4,4]{1,0:T(4,128)} %coupling.1) | copy-start | bytes 196

commit v3 on v2

--- a/solution.py
+++ b/solution.py
@@ -9,6 +9,7 @@
 STEPS = 2
 STAGES = 2 * STEPS
 HALO = 2
+VMEM_LIMIT = 66 * 1000 * 1000
 PAIR = 2
 PAD = 8
 MESH = pl.DeviceIdType.MESH
@@ -118,12 +119,17 @@
     plan,
     fields,
     velocity,
+    diffusivity_in,
+    coupling_in,
+    factor_x_in,
+    factor_y_in,
+    factor_z_in,
+    out,
     diffusivity,
     coupling,
     factor_x,
     factor_y,
     factor_z,
-    out,
     cells,
     speed,
     y_out,
@@ -307,22 +313,10 @@
             result.append(new)
         return result
 
-    def clear(condition, ref, *index):
-        @pl.when(jnp.logical_not(condition))
-        def _():
-            ref[index] = jnp.zeros_like(ref[index])
-
-    for s in range(STAGES):
-        clear(low_x, cells, s, slice(None), slice(0, 2))
-        clear(high_x, cells, s, slice(None), slice(lx + 2, lx + 4))
-        for group in range(2):
-            for side, condition in ((0, low_y), (1, high_y)):
-                clear(condition, y_in, s, group, side)
-
-    load = pltpu.make_async_copy(fields, cells.at[0, :, 2:lx + 2, rows], load_sem.at[0])
-    load.start()
-    load_speed = pltpu.make_async_copy(velocity, speed, load_sem.at[1])
-    load_speed.start()
+    def fetch(i, source, target):
+        copy = pltpu.make_async_copy(source, target, load_sem.at[i])
+        copy.start()
+        return copy
 
     partners = [
         {"gy": lax.rem(my + dy, ny), "gz": lax.rem(mz + dz, nz)}
@@ -332,6 +326,28 @@
     barrier = pltpu.get_barrier_semaphore()
     for device in partners + line:
         pl.semaphore_signal(barrier, inc=1, device_id=device, device_id_type=MESH)
+    load = fetch(0, fields, cells.at[0, :, 2:lx + 2, rows])
+    load_rest = [
+        fetch(1, velocity, speed),
+        fetch(2, diffusivity_in, diffusivity),
+        fetch(3, coupling_in, coupling),
+        fetch(4, factor_x_in, factor_x),
+        fetch(5, factor_y_in, factor_y),
+        fetch(6, factor_z_in, factor_z),
+    ]
+
+    def clear(condition, ref, *index):
+        @pl.when(jnp.logical_not(condition))
+        def _():
+            ref[index] = jnp.zeros_like(ref[index])
+
+    for s in range(STAGES):
+        clear(low_x, cells, s, slice(None), slice(0, 2))
+        clear(high_x, cells, s, slice(None), slice(lx + 2, lx + 4))
+        for group in range(2):
+            for side, condition in ((0, low_y), (1, high_y)):
+                clear(condition, y_in, s, group, side)
+
     pl.semaphore_wait(barrier, len(partners) + len(line))
 
     for v in range(nv):
@@ -347,7 +363,8 @@
 
     lax.fori_loop(0, chunks, first_pack, 0)
     start(yz_messages(0, 1, None))
-    load_speed.wait()
+    for copy in load_rest:
+        copy.wait()
     speed[...] = speed[...] * (-time_step / 12.0)
 
     def split(value):
@@ -467,13 +484,17 @@
     vmem = lambda *shape: pltpu.VMEM(shape, jnp.float32)
     dma = lambda *shape: pltpu.SemaphoreType.DMA(shape)
     whole = pl.BlockSpec(memory_space=pltpu.VMEM)
-    scalars = pl.BlockSpec(memory_space=pltpu.SMEM)
     result = pl.pallas_call(
         functools.partial(kernel, p),
         out_shape=jax.ShapeDtypeStruct((nv, p.cz, chunk_x), jnp.float32),
-        in_specs=[pl.BlockSpec(memory_space=pltpu.HBM)] * 2 + [scalars] * 2 + [whole] * 3,
+        in_specs=[pl.BlockSpec(memory_space=pl.ANY)] * 7,
         out_specs=whole,
         scratch_shapes=[
+            pltpu.SMEM(diffusivity.shape, jnp.float32),
+            pltpu.SMEM(coupling.shape, jnp.float32),
+            vmem(*factor_x.shape),
+            vmem(*factor_y.shape),
+            vmem(*factor_z.shape[::-1]),
             vmem(STAGES + 1, nv, lx + 4, ly + 2 * PAD, p.lz),
             vmem(3, lx, ly, p.lz),
             vmem(STAGES, 2, 2, nv, 8 * -(-max(4, lx - 4) // 4), p.lz),
@@ -486,7 +507,7 @@
             vmem(others, nv, p.cz, chunk_y),
             vmem(p.nx, nv, p.cz, chunk_x),
             vmem(p.nx - 1, nv, p.cz, chunk_x),
-            dma(2),
+            dma(7),
             dma(2), dma(STAGES, nv, 2),
             dma(2), dma(STAGES, nv // PAIR + 1, 2),
             dma(2), dma(STAGES, nv // PAIR + 1, 2),
@@ -494,7 +515,7 @@
             dma(p.nx - 1), dma(p.nx - 1),
         ],
         compiler_params=pltpu.CompilerParams(
-            collective_id=0, has_side_effects=True, vmem_limit_bytes=40 * 1024 * 1024),
+            collective_id=0, has_side_effects=True, vmem_limit_bytes=VMEM_LIMIT),
     )(fields, velocity, diffusivity, coupling, factor_x, factor_y, factor_z.T)
     result = result.reshape(nv, p.cz, p.ax, p.by)
     return jnp.transpose(result, (0, 2, 3, 1))

time: 41.2 us -> 36.6 us (0.89)
  local copies, waits for them, and re-layouts: 6.26 us -> 1.49 us
    unnamed x14 -> x0, local copies, waits for them, and re-layouts: 5.49 us -> none
    reshape x2, local copies, waits for them, and re-layouts: 0.77 us -> 1.49 us  [local_kernel(): result = result.reshape(nv, p.cz, p.ax, p.by)]
where the time goes in v3:
time: 36.6 us; the launch traced here: 36.4 us
  Pallas kernels  34.9 us (95%)
  local copies, waits for them, and re-layouts  1.49 us (4%)
    pallas_call x1, Pallas kernels, local_kernel(): pl.pallas_call(functools.partial(kernel, p), out_shape=jax.ShapeDtypeStru...  34.9 us
    reshape x2, local copies, waits for them, and re-layouts, local_kernel(): result = result.reshape(nv, p.cz, p.ax, p.by)  1.49 us

profile of v3, /device:TPU:0, one launch (start us, length us, event | category | flops | bytes accessed | tf_op | source)
XLA Modules:
  0.0 36.4 jit_solution(6589992653670982364)
XLA Ops:
  0.0 34.9 %shard_map.73 = f32[4,8,128]{2,1,0:T(8,128)} custom-call(f32[4,8,32,128]{3,2,1,0:T(8,128)} %fields.1, f32[3,8,32,128]{3,2,1,0:T(8,128)} %velocity.1, f32[4]{0:T(128)} %diffusivity_in.1, f32[4,4]{1,0:T(4,128)} %coupling_in.1, f32[8,32]{1,0:T(8,128)} %factor_x_in.1, f32[32,32]{1,0:T(8,128)} %factor_y_in.1, f32[32,128]{1,0:T(8,128)} %bitcast.4), custom_call_target="tpu_custom_call" | custom-call | tf_op jit(solution)/shard_map/pallas_call | solution.py:487
  34.9 0.8 %reshape.3 = f32[4,8,8,16]{3,2,1,0:T(8,128)S(1)} reshape(f32[4,8,128]{2,1,0:T(8,128)} %shard_map.73) | data formatting | bytes 32768 | tf_op jit(solution)/shard_map/reshape | solution.py:520
  35.7 0.7 %copy.10 = f32[4,8,8,16]{3,1,2,0:T(8,128)} copy(f32[4,8,8,16]{3,2,1,0:T(8,128)S(1)} %reshape.3) | data formatting | bytes 32768 | tf_op jit(solution)/shard_map/reshape | solution.py:520

commit v4 on v3

--- a/solution.py
+++ b/solution.py
@@ -10,7 +10,6 @@
 STAGES = 2 * STEPS
 HALO = 2
 VMEM_LIMIT = 66 * 1000 * 1000
-PAIR = 2
 PAD = 8
 MESH = pl.DeviceIdType.MESH
 HIGHEST = lax.Precision.HIGHEST
@@ -103,11 +102,8 @@
             self.lz == 128
             and self.ly % 8 == 0
             and min(self.nx, self.ny, self.nz) > 1
-            and self.vars % PAIR == 0
             and self.lx > 4
-            and self.lx <= 12
-            and len(self.edge) * self.tiles * 4 <= 128
-            and len(self.inner) * self.tiles * 4 <= 128
+            and self.lx * self.tiles * 4 <= 128
             and self.rank % self.nx == 0 and self.rank % self.ny == 0 and self.rank % self.nz == 0
             and self.cz % 8 == 0
             and self.lx * self.by % 128 == 0
@@ -190,33 +186,27 @@
                 x_send.at[1], x_recv.at[s, v, 1], "gx", down(mx, nx))),
         ]
 
-    chunks = nv // PAIR
-
-    def yz_messages(s, group, c):
-        if group == 0:
-            which, place = pl.ds(c * PAIR, PAIR), c
-        else:
-            which, place = slice(None), chunks
+    def yz_messages(s, v):
         result = [
             (None, None, remote(
-                z_out.at[s, group, which], z_in.at[s, group, 0, which],
-                z_send.at[0], z_recv.at[s, place, 0], "gz", up(mz, nz))),
+                z_out.at[s, v], z_in.at[s, 0, v],
+                z_send.at[0], z_recv.at[s, v, 0], "gz", up(mz, nz))),
             (None, None, remote(
-                z_out.at[s, group, which], z_in.at[s, group, 1, which],
-                z_send.at[1], z_recv.at[s, place, 1], "gz", down(mz, nz))),
+                z_out.at[s, v], z_in.at[s, 1, v],
+                z_send.at[1], z_recv.at[s, v, 1], "gz", down(mz, nz))),
         ]
         if ny == 2:
             result.append((None, None, remote(
-                y_out.at[s, group, 1 - my, which], y_in.at[s, group, my, which],
-                y_send.at[0], y_recv.at[s, place, 0], "gy", 1 - my)))
+                y_out.at[s, 1 - my, v], y_in.at[s, my, v],
+                y_send.at[0], y_recv.at[s, v, 0], "gy", 1 - my)))
         else:
             result += [
                 (high_y, low_y, remote(
-                    y_out.at[s, group, 1, which], y_in.at[s, group, 0, which],
-                    y_send.at[0], y_recv.at[s, place, 0], "gy", up(my, ny))),
+                    y_out.at[s, 1, v], y_in.at[s, 0, v],
+                    y_send.at[0], y_recv.at[s, v, 0], "gy", up(my, ny))),
                 (low_y, high_y, remote(
-                    y_out.at[s, group, 0, which], y_in.at[s, group, 1, which],
-                    y_send.at[1], y_recv.at[s, place, 1], "gy", down(my, ny))),
+                    y_out.at[s, 0, v], y_in.at[s, 1, v],
+                    y_send.at[1], y_recv.at[s, v, 1], "gy", down(my, ny))),
             ]
         return result
 
@@ -242,7 +232,7 @@
             (None, remote(z_out, z_out, z_send.at[0], z_recv.at[0, 0, 0], "gz", up(mz, nz))),
             (None, remote(z_out, z_out, z_send.at[1], z_recv.at[0, 0, 1], "gz", down(mz, nz))),
         ]
-        half = y_out.at[:, :, 0]
+        half = y_out.at[:, 0]
         if ny == 2:
             waits.append((None, remote(half, half, y_send.at[0], y_recv.at[0, 0, 0], "gy", 1 - my)))
         else:
@@ -257,36 +247,31 @@
     quarter = lax.shift_right_logical(lane, 2)
     lower = jnp.bitwise_and(lane, 3) < 2
     inside = jnp.where(lower, jnp.minimum(mz, 1), jnp.minimum(nz - 1 - mz, 1)) > 0
-    groups = (p.edge, p.inner)
-
-    def pack(s, group, v, layers):
-        z = jnp.zeros((8, 128), jnp.float32)
-        for j, value in enumerate(layers):
-            y_out[s, group, 0, v, 2 * j:2 * j + 2] = value[0:2]
-            y_out[s, group, 1, v, 2 * j:2 * j + 2] = value[ly - 2:ly]
-            for t in range(p.tiles):
-                place = 4 * (j * p.tiles + t)
-                turned = pltpu.roll(value[8 * t:8 * t + 8], (place + 2) % 128, 1)
-                z = jnp.where(quarter == j * p.tiles + t, turned, z)
-        z_out[s, group, v] = z
-
-    def advance(s, group, v):
-        edges = jnp.where(lower, z_in[s, group, 0, v], z_in[s, group, 1, v])
+
+    def pack(s, v, x, value, z):
+        y_out[s, 0, v, 2 * x:2 * x + 2] = value[0:2]
+        y_out[s, 1, v, 2 * x:2 * x + 2] = value[ly - 2:ly]
+        for t in range(p.tiles):
+            place = x * p.tiles + t
+            turned = pltpu.roll(value[8 * t:8 * t + 8], (4 * place + 2) % 128, 1)
+            z = jnp.where(quarter == place, turned, z)
+        return z
+
+    def advance(s, v, layers, z):
+        edges = jnp.where(lower, z_in[s, 0, v], z_in[s, 1, v])
         edges = jnp.where(inside, edges, 0.0)
         spread = time_step * diffusivity[v]
         rates = [time_step * coupling[v, w] for w in range(nv)]
         keep = 1.0 - 6.0 * spread
-        layers = groups[group]
-        for j, x in enumerate(layers):
-            cells[s, v, x + 2, PAD - 2:PAD] = y_in[s, group, 0, v, 2 * j:2 * j + 2]
-            cells[s, v, x + 2, PAD + ly:PAD + ly + 2] = y_in[s, group, 1, v, 2 * j:2 * j + 2]
-        result = []
-        for j, x in enumerate(layers):
+        for x in layers:
+            cells[s, v, x + 2, PAD - 2:PAD] = y_in[s, 0, v, 2 * x:2 * x + 2]
+            cells[s, v, x + 2, PAD + ly:PAD + ly + 2] = y_in[s, 1, v, 2 * x:2 * x + 2]
+        for x in layers:
             centre = cells[s, v, x + 2, rows]
             turned = [[], [], [], []]
             for t in range(p.tiles):
                 tile = centre[8 * t:8 * t + 8]
-                beside = pltpu.roll(edges, (126 - 4 * (j * p.tiles + t)) % 128, 1)
+                beside = pltpu.roll(edges, (126 - 4 * (x * p.tiles + t)) % 128, 1)
                 for i, (mask, shift) in enumerate(
                         ((lane == 0, 127), (lane == 127, 1), (lane <= 1, 126), (lane >= 126, 2))):
                     turned[i].append(pltpu.roll(jnp.where(mask, beside, tile), shift, 1))
@@ -310,8 +295,9 @@
             if s % 2 == 1:
                 new = 0.5 * (new + cells[s - 1, v, x + 2, rows])
             cells[s + 1, v, x + 2, rows] = new
-            result.append(new)
-        return result
+            if s + 1 < STAGES:
+                z = pack(s + 1, v, x, new, z)
+        return z
 
     def fetch(i, source, target):
         copy = pltpu.make_async_copy(source, target, load_sem.at[i])
@@ -344,9 +330,8 @@
     for s in range(STAGES):
         clear(low_x, cells, s, slice(None), slice(0, 2))
         clear(high_x, cells, s, slice(None), slice(lx + 2, lx + 4))
-        for group in range(2):
-            for side, condition in ((0, low_y), (1, high_y)):
-                clear(condition, y_in, s, group, side)
+        clear(low_y, y_in, s, 0)
+        clear(high_y, y_in, s, 1)
 
     pl.semaphore_wait(barrier, len(partners) + len(line))
 
@@ -354,15 +339,17 @@
         start(x_messages(0, v))
     load.wait()
 
-    def first_pack(c, carry):
-        for v in (c * PAIR + i for i in range(PAIR)):
-            for group in range(2):
-                pack(0, group, v, [cells[0, v, x + 2, rows] for x in groups[group]])
-        start(yz_messages(0, 0, c))
+    blank = jnp.zeros((8, 128), jnp.float32)
+
+    def first_pack(v, carry):
+        z = blank
+        for x in range(lx):
+            z = pack(0, v, x, cells[0, v, x + 2, rows], z)
+        z_out[0, v] = z
+        start(yz_messages(0, v))
         return carry
 
-    lax.fori_loop(0, chunks, first_pack, 0)
-    start(yz_messages(0, 1, None))
+    lax.fori_loop(0, nv, first_pack, 0)
     for copy in load_rest:
         copy.wait()
     speed[...] = speed[...] * (-time_step / 12.0)
@@ -411,36 +398,20 @@
                     yz_out[y * nz + z, v] = reduced[
                         z * p.cz:(z + 1) * p.cz, y * chunk_y:(y + 1) * chunk_y]
 
-        def edge_part(c, carry):
-            for i in range(PAIR):
-                v = c * PAIR + i
-                if i == 0:
-                    arrive(yz_messages(s, 0, c))
-                arrive(x_messages(s, v))
-                layers = advance(s, 0, v)
-                if last:
-                    project(v)
-                else:
-                    start(x_messages(s + 1, v))
-                    pack(s + 1, 0, v, layers)
+        def stage(v, carry):
+            arrive(yz_messages(s, v) + x_messages(s, v))
+            z = advance(s, v, p.edge, blank)
             if not last:
-                start(yz_messages(s + 1, 0, c))
+                start(x_messages(s + 1, v))
+            z = advance(s, v, p.inner, z)
+            if last:
+                project(v)
+            else:
+                z_out[s + 1, v] = z
+                start(yz_messages(s + 1, v))
             return carry
 
-        def inner_part(v, carry):
-            layers = advance(s, 1, v)
-            if not last:
-                pack(s + 1, 1, v, layers)
-            return carry
-
-        if not last:
-            lax.fori_loop(0, chunks, edge_part, 0)
-        arrive(yz_messages(s, 1, None))
-        lax.fori_loop(0, nv, inner_part, 0)
-        if not last:
-            start(yz_messages(s + 1, 1, None))
-        else:
-            lax.fori_loop(0, chunks, edge_part, 0)
+        lax.fori_loop(0, nv, stage, 0)
 
     plane = []
     for i, device in enumerate(partners):
@@ -469,7 +440,8 @@
     for i, copy in enumerate(along):
         copy.wait_recv()
         total = total + x_in[i]
-    out[...] = total
+    for a in range(p.ax):
+        out[:, a] = total[:, :, a * p.by:(a + 1) * p.by]
 
     all_sent()
     for copy in plane + along:
@@ -486,7 +458,7 @@
     whole = pl.BlockSpec(memory_space=pltpu.VMEM)
     result = pl.pallas_call(
         functools.partial(kernel, p),
-        out_shape=jax.ShapeDtypeStruct((nv, p.cz, chunk_x), jnp.float32),
+        out_shape=jax.ShapeDtypeStruct((nv, p.ax, p.cz, p.by), jnp.float32),
         in_specs=[pl.BlockSpec(memory_space=pl.ANY)] * 7,
         out_specs=whole,
         scratch_shapes=[
@@ -497,10 +469,10 @@
             vmem(*factor_z.shape[::-1]),
             vmem(STAGES + 1, nv, lx + 4, ly + 2 * PAD, p.lz),
             vmem(3, lx, ly, p.lz),
-            vmem(STAGES, 2, 2, nv, 8 * -(-max(4, lx - 4) // 4), p.lz),
-            vmem(STAGES, 2, 2, nv, 8 * -(-max(4, lx - 4) // 4), p.lz),
+            vmem(STAGES, 2, nv, 8 * -(-lx // 4), p.lz),
+            vmem(STAGES, 2, nv, 8 * -(-lx // 4), p.lz),
+            vmem(STAGES, nv, 8, 128),
             vmem(STAGES, 2, nv, 8, 128),
-            vmem(STAGES, 2, 2, nv, 8, 128),
             pltpu.VMEM((2, lx * ly, p.ny * chunk_y), jnp.bfloat16),
             pltpu.VMEM((2, chunk_y, p.nx * chunk_x), jnp.bfloat16),
             vmem(p.ny * p.nz, nv, p.cz, chunk_y),
@@ -509,16 +481,15 @@
             vmem(p.nx - 1, nv, p.cz, chunk_x),
             dma(7),
             dma(2), dma(STAGES, nv, 2),
-            dma(2), dma(STAGES, nv // PAIR + 1, 2),
-            dma(2), dma(STAGES, nv // PAIR + 1, 2),
+            dma(2), dma(STAGES, nv, 2),
+            dma(2), dma(STAGES, nv, 2),
             dma(others), dma(others),
             dma(p.nx - 1), dma(p.nx - 1),
         ],
         compiler_params=pltpu.CompilerParams(
             collective_id=0, has_side_effects=True, vmem_limit_bytes=VMEM_LIMIT),
     )(fields, velocity, diffusivity, coupling, factor_x, factor_y, factor_z.T)
-    result = result.reshape(nv, p.cz, p.ax, p.by)
-    return jnp.transpose(result, (0, 2, 3, 1))
+    return jnp.transpose(result, (0, 1, 3, 2))
 
 
 def solution(mesh):

time: 36.6 us -> 33.4 us (0.913)
  Pallas kernels: 34.9 us -> 31.7 us
    pallas_call x1, Pallas kernels: 34.9 us -> 31.7 us  [local_kernel(): pl.pallas_call(functools.partial(kernel, p), out_shape=jax.ShapeDtypeStru...]
    unnamed x0 -> x1, local copies, waits for them, and re-layouts: none -> 1.57 us
    reshape x2 -> x0, local copies, waits for them, and re-layouts: 1.49 us -> none  [local_kernel(): result = result.reshape(nv, p.cz, p.ax, p.by)]
where the time goes in v4:
time: 33.4 us; the launch traced here: 33.2 us
  Pallas kernels  31.7 us (95%)
  local copies, waits for them, and re-layouts  1.57 us (5%)
    pallas_call x1, Pallas kernels, local_kernel(): pl.pallas_call(functools.partial(kernel, p), out_shape=jax.ShapeDtypeStru...  31.7 us
    unnamed x1, local copies, waits for them, and re-layouts  1.57 us

profile of v4, /device:TPU:0, one launch (start us, length us, event | category | flops | bytes accessed | tf_op | source)
XLA Modules:
  0.0 33.2 jit_solution(5688436428526334915)
XLA Ops:
  0.0 31.7 %shard_map.73 = f32[4,8,8,16]{3,2,1,0:T(8,128)} custom-call(f32[4,8,32,128]{3,2,1,0:T(8,128)} %fields.1, f32[3,8,32,128]{3,2,1,0:T(8,128)} %velocity.1, f32[4]{0:T(128)} %diffusivity_in.1, f32[4,4]{1,0:T(4,128)} %coupling_in.1, f32[8,32]{1,0:T(8,128)} %factor_x_in.1, f32[32,32]{1,0:T(8,128)} %factor_y_in.1, f32[32,128]{1,0:T(8,128)} %bitcast.3), custom_call_target="tpu_custom_call" | custom-call | tf_op jit(solution)/shard_map/pallas_call | solution.py:459
  31.7 1.6 %copy.9 = f32[4,8,16,8]{2,3,1,0:T(8,128)} copy(f32[4,8,16,8]{2,3,1,0:T(8,128)} %bitcast.2) | data formatting | bytes 32768

commit v5 on v4

--- a/solution.py
+++ b/solution.py
@@ -10,7 +10,6 @@
 STAGES = 2 * STEPS
 HALO = 2
 VMEM_LIMIT = 66 * 1000 * 1000
-PAD = 8
 MESH = pl.DeviceIdType.MESH
 HIGHEST = lax.Precision.HIGHEST
 
@@ -101,6 +100,7 @@
         return (
             self.lz == 128
             and self.ly % 8 == 0
+            and self.ly >= 16
             and min(self.nx, self.ny, self.nz) > 1
             and self.lx > 4
             and self.lx * self.tiles * 4 <= 128
@@ -126,6 +126,8 @@
     factor_x,
     factor_y,
     factor_z,
+    raw,
+    raw_speed,
     cells,
     speed,
     y_out,
@@ -154,7 +156,7 @@
     nx, ny, nz = p.nx, p.ny, p.nz
     lx, ly, nv = p.lx, p.ly, p.vars
     mx, my, mz = lax.axis_index("gx"), lax.axis_index("gy"), lax.axis_index("gz")
-    rows = slice(PAD, PAD + ly)
+    tiles = p.tiles
     low_x, high_x = mx > 0, mx < nx - 1
     low_y, high_y = my > 0, my < ny - 1
     low_z, high_z = mz > 0, mz < nz - 1
@@ -174,16 +176,15 @@
     def x_messages(s, v):
         if s == 0:
             top, bottom = fields.at[v, lx - 2:lx], fields.at[v, 0:2]
+            below, above = raw.at[v, 0:2], raw.at[v, lx + 2:lx + 4]
         else:
-            top = cells.at[s, v, lx:lx + 2, rows]
-            bottom = cells.at[s, v, 2:4, rows]
+            top, bottom = cells.at[s, v, lx:lx + 2], cells.at[s, v, 2:4]
+            below, above = cells.at[s, v, 0:2], cells.at[s, v, lx + 2:lx + 4]
         return [
             (high_x, low_x, remote(
-                top, cells.at[s, v, 0:2, rows],
-                x_send.at[0], x_recv.at[s, v, 0], "gx", up(mx, nx))),
+                top, below, x_send.at[0], x_recv.at[s, v, 0], "gx", up(mx, nx))),
             (low_x, high_x, remote(
-                bottom, cells.at[s, v, lx + 2:lx + 4, rows],
-                x_send.at[1], x_recv.at[s, v, 1], "gx", down(mx, nx))),
+                bottom, above, x_send.at[1], x_recv.at[s, v, 1], "gx", down(mx, nx))),
         ]
 
     def yz_messages(s, v):
@@ -225,7 +226,7 @@
             guarded(gets, copy.wait_recv)
 
     def all_sent():
-        layers = cells.at[0:STAGES, :, 0:2, rows]
+        layers = cells.at[0:STAGES, :, 0:2]
         waits = [
             (high_x, remote(layers, layers, x_send.at[0], x_recv.at[0, 0, 0], "gx", up(mx, nx))),
             (low_x, remote(layers, layers, x_send.at[1], x_recv.at[0, 0, 1], "gx", down(mx, nx))),
@@ -244,16 +245,18 @@
             guarded(condition, copy.wait_send)
 
     lane = lax.broadcasted_iota(jnp.int32, (8, 128), 1)
+    sublane = lax.broadcasted_iota(jnp.int32, (8, 128), 0)
     quarter = lax.shift_right_logical(lane, 2)
     lower = jnp.bitwise_and(lane, 3) < 2
     inside = jnp.where(lower, jnp.minimum(mz, 1), jnp.minimum(nz - 1 - mz, 1)) > 0
 
     def pack(s, v, x, value, z):
-        y_out[s, 0, v, 2 * x:2 * x + 2] = value[0:2]
-        y_out[s, 1, v, 2 * x:2 * x + 2] = value[ly - 2:ly]
+        for i in range(2):
+            y_out[s, 0, v, 2 * x + i:2 * x + i + 1] = value[i, 0:1]
+            y_out[s, 1, v, 2 * x + i:2 * x + i + 1] = value[tiles - 2 + i, 7:8]
         for t in range(p.tiles):
             place = x * p.tiles + t
-            turned = pltpu.roll(value[8 * t:8 * t + 8], (4 * place + 2) % 128, 1)
+            turned = pltpu.roll(value[t], (4 * place + 2) % 128, 1)
             z = jnp.where(quarter == place, turned, z)
         return z
 
@@ -264,23 +267,26 @@
         rates = [time_step * coupling[v, w] for w in range(nv)]
         keep = 1.0 - 6.0 * spread
         for x in layers:
-            cells[s, v, x + 2, PAD - 2:PAD] = y_in[s, 0, v, 2 * x:2 * x + 2]
-            cells[s, v, x + 2, PAD + ly:PAD + ly + 2] = y_in[s, 1, v, 2 * x:2 * x + 2]
-        for x in layers:
-            centre = cells[s, v, x + 2, rows]
+            centre = cells[s, v, x + 2]
+            along = [
+                jnp.where(sublane == 0, y_in[s, 0, v, 2 * x + i:2 * x + i + 1],
+                          pltpu.roll(centre[tiles - 2 + i], 1, 0)) for i in range(2)
+            ] + [centre[t] for t in range(tiles)] + [
+                jnp.where(sublane == 7, y_in[s, 1, v, 2 * x + i:2 * x + i + 1],
+                          pltpu.roll(centre[i], 7, 0)) for i in range(2)
+            ]
+            shifted = lambda offset: jnp.stack(along[2 + offset:2 + offset + tiles])
             turned = [[], [], [], []]
             for t in range(p.tiles):
-                tile = centre[8 * t:8 * t + 8]
+                tile = centre[t]
                 beside = pltpu.roll(edges, (126 - 4 * (x * p.tiles + t)) % 128, 1)
                 for i, (mask, shift) in enumerate(
                         ((lane == 0, 127), (lane == 127, 1), (lane <= 1, 126), (lane >= 126, 2))):
                     turned[i].append(pltpu.roll(jnp.where(mask, beside, tile), shift, 1))
             near = [
-                (cells[s, v, x + 3, rows], cells[s, v, x + 1, rows],
-                 cells[s, v, x + 4, rows], cells[s, v, x, rows]),
-                (cells[s, v, x + 2, PAD + 1:PAD + 1 + ly], cells[s, v, x + 2, PAD - 1:PAD - 1 + ly],
-                 cells[s, v, x + 2, PAD + 2:PAD + 2 + ly], cells[s, v, x + 2, PAD - 2:PAD - 2 + ly]),
-                tuple(jnp.concatenate(parts, axis=0) for parts in turned),
+                (cells[s, v, x + 3], cells[s, v, x + 1], cells[s, v, x + 4], cells[s, v, x]),
+                (shifted(1), shifted(-1), shifted(2), shifted(-2)),
+                tuple(jnp.stack(parts) for parts in turned),
             ]
             moved = around = None
             for a, (next1, last1, next2, last2) in enumerate(near):
@@ -290,11 +296,11 @@
                 around = both if around is None else around + both
             factor = keep
             for w in range(nv):
-                factor = factor + rates[w] * cells[s, w, x + 2, rows]
+                factor = factor + rates[w] * cells[s, w, x + 2]
             new = centre * factor + moved + spread * around
             if s % 2 == 1:
-                new = 0.5 * (new + cells[s - 1, v, x + 2, rows])
-            cells[s + 1, v, x + 2, rows] = new
+                new = 0.5 * (new + cells[s - 1, v, x + 2])
+            cells[s + 1, v, x + 2] = new
             if s + 1 < STAGES:
                 z = pack(s + 1, v, x, new, z)
         return z
@@ -312,9 +318,9 @@
     barrier = pltpu.get_barrier_semaphore()
     for device in partners + line:
         pl.semaphore_signal(barrier, inc=1, device_id=device, device_id_type=MESH)
-    load = fetch(0, fields, cells.at[0, :, 2:lx + 2, rows])
+    load = fetch(0, fields, raw.at[:, 2:lx + 2])
     load_rest = [
-        fetch(1, velocity, speed),
+        fetch(1, velocity, raw_speed),
         fetch(2, diffusivity_in, diffusivity),
         fetch(3, coupling_in, coupling),
         fetch(4, factor_x_in, factor_x),
@@ -328,8 +334,10 @@
             ref[index] = jnp.zeros_like(ref[index])
 
     for s in range(STAGES):
-        clear(low_x, cells, s, slice(None), slice(0, 2))
-        clear(high_x, cells, s, slice(None), slice(lx + 2, lx + 4))
+        edge = cells if s else raw
+        lead = (s,) if s else ()
+        clear(low_x, edge, *lead, slice(None), slice(0, 2))
+        clear(high_x, edge, *lead, slice(None), slice(lx + 2, lx + 4))
         clear(low_y, y_in, s, 0)
         clear(high_y, y_in, s, 1)
 
@@ -341,10 +349,15 @@
 
     blank = jnp.zeros((8, 128), jnp.float32)
 
+    def arrange(v, x):
+        for t in range(tiles):
+            cells[0, v, x, t] = raw[v, x, pl.ds(t, 8, stride=tiles)]
+
     def first_pack(v, carry):
         z = blank
         for x in range(lx):
-            z = pack(0, v, x, cells[0, v, x + 2, rows], z)
+            arrange(v, x + 2)
+            z = pack(0, v, x, cells[0, v, x + 2], z)
         z_out[0, v] = z
         start(yz_messages(0, v))
         return carry
@@ -352,7 +365,14 @@
     lax.fori_loop(0, nv, first_pack, 0)
     for copy in load_rest:
         copy.wait()
-    speed[...] = speed[...] * (-time_step / 12.0)
+
+    def arrange_speed(a, carry):
+        for x in range(lx):
+            for t in range(tiles):
+                speed[a, x, t] = raw_speed[a, x, pl.ds(t, 8, stride=tiles)] * (-time_step / 12.0)
+        return carry
+
+    lax.fori_loop(0, 3, arrange_speed, 0)
 
     def split(value):
         high = value.astype(jnp.bfloat16)
@@ -369,7 +389,11 @@
     column = lax.broadcasted_iota(jnp.int32, (p.rank, wide_y), 1)
     row = lax.broadcasted_iota(jnp.int32, (p.rank, wide_y), 0)
     place_y = jnp.where(row == column // chunk_y * p.by + column % p.by, 1.0, 0.0)
-    repeated = jnp.dot(factor_y[...], place_y, precision=HIGHEST, preferred_element_type=jnp.float32)
+    column = lax.broadcasted_iota(jnp.int32, (ly, ly), 1)
+    row = lax.broadcasted_iota(jnp.int32, (ly, ly), 0)
+    order = jnp.where(column == row % 8 * tiles + row // 8, 1.0, 0.0)
+    ordered = jnp.dot(order, factor_y[...], precision=HIGHEST, preferred_element_type=jnp.float32)
+    repeated = jnp.dot(ordered, place_y, precision=HIGHEST, preferred_element_type=jnp.float32)
     column = lax.broadcasted_iota(jnp.int32, (ly, wide_y), 1) % chunk_y // p.by
     for x in range(lx):
         for i, part in enumerate(split(jnp.where(column == x, repeated, 0.0))):
@@ -390,7 +414,7 @@
         last = s == STAGES - 1
 
         def project(v):
-            state = cells[STAGES, v, 2:lx + 2, rows].reshape(lx * ly, p.lz)
+            state = cells[STAGES, v, 2:lx + 2].reshape(lx * ly, p.lz)
             reduced = product(split(factor_z[...]), split(state), ((1,), (1,)))
             reduced = product(split(reduced), (spread_y[0], spread_y[1]))
             for y in range(ny):
@@ -400,6 +424,9 @@
 
         def stage(v, carry):
             arrive(yz_messages(s, v) + x_messages(s, v))
+            if s == 0:
+                for x in (0, 1, lx + 2, lx + 3):
+                    arrange(v, x)
             z = advance(s, v, p.edge, blank)
             if not last:
                 start(x_messages(s + 1, v))
@@ -467,8 +494,10 @@
             vmem(*factor_x.shape),
             vmem(*factor_y.shape),
             vmem(*factor_z.shape[::-1]),
-            vmem(STAGES + 1, nv, lx + 4, ly + 2 * PAD, p.lz),
+            vmem(nv, lx + 4, ly, p.lz),
             vmem(3, lx, ly, p.lz),
+            vmem(STAGES + 1, nv, lx + 4, p.tiles, 8, p.lz),
+            vmem(3, lx, p.tiles, 8, p.lz),
             vmem(STAGES, 2, nv, 8 * -(-lx // 4), p.lz),
             vmem(STAGES, 2, nv, 8 * -(-lx // 4), p.lz),
             vmem(STAGES, nv, 8, 128),

time: 33.4 us -> 33.4 us (level)
  no operation moved by 1% of the time
where the time goes in v5:
time: 33.4 us; the launch traced here: 33.2 us
  Pallas kernels  31.7 us (95%)
  local copies, waits for them, and re-layouts  1.57 us (5%)
    pallas_call x1, Pallas kernels, local_kernel(): pl.pallas_call(functools.partial(kernel, p), out_shape=jax.ShapeDtypeStru...  31.7 us
    unnamed x1, local copies, waits for them, and re-layouts  1.57 us

profile of v5, /device:TPU:0, one launch (start us, length us, event | category | flops | bytes accessed | tf_op | source)
XLA Modules:
  0.0 33.2 jit_solution(4432377624692791743)
XLA Ops:
  0.0 31.7 %shard_map.73 = f32[4,8,8,16]{3,2,1,0:T(8,128)} custom-call(f32[4,8,32,128]{3,2,1,0:T(8,128)} %fields.1, f32[3,8,32,128]{3,2,1,0:T(8,128)} %velocity.1, f32[4]{0:T(128)} %diffusivity_in.1, f32[4,4]{1,0:T(4,128)} %coupling_in.1, f32[8,32]{1,0:T(8,128)} %factor_x_in.1, f32[32,32]{1,0:T(8,128)} %factor_y_in.1, f32[32,128]{1,0:T(8,128)} %bitcast.3), custom_call_target="tpu_custom_call" | custom-call | tf_op jit(solution)/shard_map/pallas_call | solution.py:486
  31.7 1.6 %copy.9 = f32[4,8,16,8]{2,3,1,0:T(8,128)} copy(f32[4,8,16,8]{2,3,1,0:T(8,128)} %bitcast.2) | data formatting | bytes 32768

commit v6 on v5

--- a/solution.py
+++ b/solution.py
@@ -410,6 +410,13 @@
         for i, part in enumerate(split(jnp.where(column == row, repeated[x:x + 1], 0.0))):
             spread_x[i, x * p.by:(x + 1) * p.by] = part
 
+    def plane_message(i, which):
+        device = partners[i]
+        return pltpu.make_async_remote_copy(
+            src_ref=yz_out.at[device["gy"] * nz + device["gz"], which], dst_ref=yz_in.at[i, which],
+            send_sem=yz_send.at[i], recv_sem=yz_recv.at[i],
+            device_id=device, device_id_type=MESH)
+
     for s in range(STAGES):
         last = s == STAGES - 1
 
@@ -433,6 +440,8 @@
             z = advance(s, v, p.inner, z)
             if last:
                 project(v)
+                for i in range(len(partners)):
+                    plane_message(i, v).start()
             else:
                 z_out[s + 1, v] = z
                 start(yz_messages(s + 1, v))
@@ -440,13 +449,7 @@
 
         lax.fori_loop(0, nv, stage, 0)
 
-    plane = []
-    for i, device in enumerate(partners):
-        plane.append(pltpu.make_async_remote_copy(
-            src_ref=yz_out.at[device["gy"] * nz + device["gz"]], dst_ref=yz_in.at[i],
-            send_sem=yz_send.at[i], recv_sem=yz_recv.at[i],
-            device_id=device, device_id_type=MESH))
-        plane[-1].start()
+    plane = [plane_message(i, slice(None)) for i in range(len(partners))]
     total = yz_out[my * nz + mz]
     for i, copy in enumerate(plane):
         copy.wait_recv()
@@ -485,7 +488,7 @@
     whole = pl.BlockSpec(memory_space=pltpu.VMEM)
     result = pl.pallas_call(
         functools.partial(kernel, p),
-        out_shape=jax.ShapeDtypeStruct((nv, p.ax, p.cz, p.by), jnp.float32),
+        out_shape=pltpu.VMEM((nv, p.ax, p.cz, p.by), jnp.float32),
         in_specs=[pl.BlockSpec(memory_space=pl.ANY)] * 7,
         out_specs=whole,
         scratch_shapes=[

time: 33.4 us -> 31.4 us (0.940)
  Pallas kernels: 31.7 us -> 30.6 us
  local copies, waits for them, and re-layouts: 1.57 us -> 0.66 us
    pallas_call x1, Pallas kernels: 31.7 us -> 30.6 us  [local_kernel(): pl.pallas_call(functools.partial(kernel, p), out_shape=pltpu.VMEM((nv, p....]
    unnamed x1, local copies, waits for them, and re-layouts: 1.57 us -> 0.66 us
where the time goes in v6:
time: 31.4 us; the launch traced here: 31.3 us
  Pallas kernels  30.6 us (97%)
  local copies, waits for them, and re-layouts  0.66 us (2%)
    pallas_call x1, Pallas kernels, local_kernel(): pl.pallas_call(functools.partial(kernel, p), out_shape=pltpu.VMEM((nv, p....  30.6 us
    unnamed x1, local copies, waits for them, and re-layouts  0.66 us

profile of v6, /device:TPU:0, one launch (start us, length us, event | category | flops | bytes accessed | tf_op | source)
XLA Modules:
  0.0 31.3 jit_solution(1671204426080921093)
XLA Ops:
  0.0 30.6 %shard_map.73 = f32[4,8,8,16]{3,2,1,0:T(8,128)S(1)} custom-call(f32[4,8,32,128]{3,2,1,0:T(8,128)} %fields.1, f32[3,8,32,128]{3,2,1,0:T(8,128)} %velocity.1, f32[4]{0:T(128)} %diffusivity_in.1, f32[4,4]{1,0:T(4,128)} %coupling_in.1, f32[8,32]{1,0:T(8,128)} %factor_x_in.1, f32[32,32]{1,0:T(8,128)} %factor_y_in.1, f32[32,128]{1,0:T(8,128)} %bitcast.3), custom_call_target="tpu_custom_call" | custom-call | tf_op jit(solution)/shard_map/pallas_call | solution.py:489
  30.6 0.7 %copy.9 = f32[4,8,16,8]{2,3,1,0:T(8,128)} copy(f32[4,8,16,8]{2,3,1,0:T(8,128)S(1)} %bitcast.2) | data formatting | bytes 32768

commit v7 on v6

--- a/solution.py
+++ b/solution.py
@@ -9,6 +9,7 @@
 STEPS = 2
 STAGES = 2 * STEPS
 HALO = 2
+GROUP = 2
 VMEM_LIMIT = 66 * 1000 * 1000
 MESH = pl.DeviceIdType.MESH
 HIGHEST = lax.Precision.HIGHEST
@@ -102,6 +103,7 @@
             and self.ly % 8 == 0
             and self.ly >= 16
             and min(self.nx, self.ny, self.nz) > 1
+            and self.vars % GROUP == 0
             and self.lx > 4
             and self.lx * self.tiles * 4 <= 128
             and self.rank % self.nx == 0 and self.rank % self.ny == 0 and self.rank % self.nz == 0
@@ -173,7 +175,8 @@
     def down(index, count):
         return lax.rem(index + count - 1, count)
 
-    def x_messages(s, v):
+    def x_messages(s, c):
+        v = pl.ds(c * GROUP, GROUP)
         if s == 0:
             top, bottom = fields.at[v, lx - 2:lx], fields.at[v, 0:2]
             below, above = raw.at[v, 0:2], raw.at[v, lx + 2:lx + 4]
@@ -182,32 +185,33 @@
             below, above = cells.at[s, v, 0:2], cells.at[s, v, lx + 2:lx + 4]
         return [
             (high_x, low_x, remote(
-                top, below, x_send.at[0], x_recv.at[s, v, 0], "gx", up(mx, nx))),
+                top, below, x_send.at[0], x_recv.at[s, c, 0], "gx", up(mx, nx))),
             (low_x, high_x, remote(
-                bottom, above, x_send.at[1], x_recv.at[s, v, 1], "gx", down(mx, nx))),
+                bottom, above, x_send.at[1], x_recv.at[s, c, 1], "gx", down(mx, nx))),
         ]
 
-    def yz_messages(s, v):
+    def yz_messages(s, c):
+        v = pl.ds(c * GROUP, GROUP)
         result = [
             (None, None, remote(
                 z_out.at[s, v], z_in.at[s, 0, v],
-                z_send.at[0], z_recv.at[s, v, 0], "gz", up(mz, nz))),
+                z_send.at[0], z_recv.at[s, c, 0], "gz", up(mz, nz))),
             (None, None, remote(
                 z_out.at[s, v], z_in.at[s, 1, v],
-                z_send.at[1], z_recv.at[s, v, 1], "gz", down(mz, nz))),
+                z_send.at[1], z_recv.at[s, c, 1], "gz", down(mz, nz))),
         ]
         if ny == 2:
             result.append((None, None, remote(
                 y_out.at[s, 1 - my, v], y_in.at[s, my, v],
-                y_send.at[0], y_recv.at[s, v, 0], "gy", 1 - my)))
+                y_send.at[0], y_recv.at[s, c, 0], "gy", 1 - my)))
         else:
             result += [
                 (high_y, low_y, remote(
                     y_out.at[s, 1, v], y_in.at[s, 0, v],
-                    y_send.at[0], y_recv.at[s, v, 0], "gy", up(my, ny))),
+                    y_send.at[0], y_recv.at[s, c, 0], "gy", up(my, ny))),
                 (low_y, high_y, remote(
                     y_out.at[s, 0, v], y_in.at[s, 1, v],
-                    y_send.at[1], y_recv.at[s, v, 1], "gy", down(my, ny))),
+                    y_send.at[1], y_recv.at[s, c, 1], "gy", down(my, ny))),
             ]
         return result
 
@@ -260,50 +264,65 @@
             z = jnp.where(quarter == place, turned, z)
         return z
 
-    def advance(s, v, layers, z):
+    def advance(s, c, layers, packed):
+        packed = list(packed)
+        variables = [c * GROUP + i for i in range(GROUP)]
+        terms = [coefficients(s, v) for v in variables]
+        ready = []
+        for x in layers:
+            values = [cells[s, w, x + 2] for w in range(nv)]
+            speeds = [speed[a, x] for a in range(3)]
+            for i, v in enumerate(variables):
+                ready.append((i, v, x, advance_layer(s, v, x, terms[i], values, speeds)))
+        for i, v, x, new in ready:
+            cells[s + 1, v, x + 2] = new
+            if s + 1 < STAGES:
+                packed[i] = pack(s + 1, v, x, new, packed[i])
+        return packed
+
+    def coefficients(s, v):
         edges = jnp.where(lower, z_in[s, 0, v], z_in[s, 1, v])
         edges = jnp.where(inside, edges, 0.0)
         spread = time_step * diffusivity[v]
         rates = [time_step * coupling[v, w] for w in range(nv)]
-        keep = 1.0 - 6.0 * spread
-        for x in layers:
-            centre = cells[s, v, x + 2]
-            along = [
-                jnp.where(sublane == 0, y_in[s, 0, v, 2 * x + i:2 * x + i + 1],
-                          pltpu.roll(centre[tiles - 2 + i], 1, 0)) for i in range(2)
-            ] + [centre[t] for t in range(tiles)] + [
-                jnp.where(sublane == 7, y_in[s, 1, v, 2 * x + i:2 * x + i + 1],
-                          pltpu.roll(centre[i], 7, 0)) for i in range(2)
-            ]
-            shifted = lambda offset: jnp.stack(along[2 + offset:2 + offset + tiles])
-            turned = [[], [], [], []]
-            for t in range(p.tiles):
-                tile = centre[t]
-                beside = pltpu.roll(edges, (126 - 4 * (x * p.tiles + t)) % 128, 1)
-                for i, (mask, shift) in enumerate(
-                        ((lane == 0, 127), (lane == 127, 1), (lane <= 1, 126), (lane >= 126, 2))):
-                    turned[i].append(pltpu.roll(jnp.where(mask, beside, tile), shift, 1))
-            near = [
-                (cells[s, v, x + 3], cells[s, v, x + 1], cells[s, v, x + 4], cells[s, v, x]),
-                (shifted(1), shifted(-1), shifted(2), shifted(-2)),
-                tuple(jnp.stack(parts) for parts in turned),
-            ]
-            moved = around = None
-            for a, (next1, last1, next2, last2) in enumerate(near):
-                flow = speed[a, x] * (8.0 * (next1 - last1) - (next2 - last2))
-                both = next1 + last1
-                moved = flow if moved is None else moved + flow
-                around = both if around is None else around + both
-            factor = keep
-            for w in range(nv):
-                factor = factor + rates[w] * cells[s, w, x + 2]
-            new = centre * factor + moved + spread * around
-            if s % 2 == 1:
-                new = 0.5 * (new + cells[s - 1, v, x + 2])
-            cells[s + 1, v, x + 2] = new
-            if s + 1 < STAGES:
-                z = pack(s + 1, v, x, new, z)
-        return z
+        return edges, spread, rates, 1.0 - 6.0 * spread
+
+    def advance_layer(s, v, x, term, values, speeds):
+        edges, spread, rates, keep = term
+        centre = cells[s, v, x + 2]
+        along = [
+            jnp.where(sublane == 0, y_in[s, 0, v, 2 * x + i:2 * x + i + 1],
+                      pltpu.roll(centre[tiles - 2 + i], 1, 0)) for i in range(2)
+        ] + [centre[t] for t in range(tiles)] + [
+            jnp.where(sublane == 7, y_in[s, 1, v, 2 * x + i:2 * x + i + 1],
+                      pltpu.roll(centre[i], 7, 0)) for i in range(2)
+        ]
+        shifted = lambda offset: jnp.stack(along[2 + offset:2 + offset + tiles])
+        turned = [[], [], [], []]
+        for t in range(p.tiles):
+            tile = centre[t]
+            beside = pltpu.roll(edges, (126 - 4 * (x * p.tiles + t)) % 128, 1)
+            for i, (mask, shift) in enumerate(
+                    ((lane == 0, 127), (lane == 127, 1), (lane <= 1, 126), (lane >= 126, 2))):
+                turned[i].append(pltpu.roll(jnp.where(mask, beside, tile), shift, 1))
+        near = [
+            (cells[s, v, x + 3], cells[s, v, x + 1], cells[s, v, x + 4], cells[s, v, x]),
+            (shifted(1), shifted(-1), shifted(2), shifted(-2)),
+            tuple(jnp.stack(parts) for parts in turned),
+        ]
+        moved = around = None
+        for a, (next1, last1, next2, last2) in enumerate(near):
+            flow = speeds[a] * (8.0 * (next1 - last1) - (next2 - last2))
+            both = next1 + last1
+            moved = flow if moved is None else moved + flow
+            around = both if around is None else around + both
+        factor = keep
+        for w in range(nv):
+            factor = factor + rates[w] * values[w]
+        new = centre * factor + moved + spread * around
+        if s % 2 == 1:
+            new = 0.5 * (new + cells[s - 1, v, x + 2])
+        return new
 
     def fetch(i, source, target):
         copy = pltpu.make_async_copy(source, target, load_sem.at[i])
@@ -343,8 +362,8 @@
 
     pl.semaphore_wait(barrier, len(partners) + len(line))
 
-    for v in range(nv):
-        start(x_messages(0, v))
+    for c in range(nv // GROUP):
+        start(x_messages(0, c))
     load.wait()
 
     blank = jnp.zeros((8, 128), jnp.float32)
@@ -353,16 +372,17 @@
         for t in range(tiles):
             cells[0, v, x, t] = raw[v, x, pl.ds(t, 8, stride=tiles)]
 
-    def first_pack(v, carry):
-        z = blank
-        for x in range(lx):
-            arrange(v, x + 2)
-            z = pack(0, v, x, cells[0, v, x + 2], z)
-        z_out[0, v] = z
-        start(yz_messages(0, v))
+    def first_pack(c, carry):
+        for v in (c * GROUP + i for i in range(GROUP)):
+            z = blank
+            for x in range(lx):
+                arrange(v, x + 2)
+                z = pack(0, v, x, cells[0, v, x + 2], z)
+            z_out[0, v] = z
+        start(yz_messages(0, c))
         return carry
 
-    lax.fori_loop(0, nv, first_pack, 0)
+    lax.fori_loop(0, nv // GROUP, first_pack, 0)
     for copy in load_rest:
         copy.wait()
 
@@ -429,25 +449,29 @@
                     yz_out[y * nz + z, v] = reduced[
                         z * p.cz:(z + 1) * p.cz, y * chunk_y:(y + 1) * chunk_y]
 
-        def stage(v, carry):
-            arrive(yz_messages(s, v) + x_messages(s, v))
+        def stage(c, carry):
+            variables = [c * GROUP + i for i in range(GROUP)]
+            arrive(yz_messages(s, c) + x_messages(s, c))
             if s == 0:
-                for x in (0, 1, lx + 2, lx + 3):
-                    arrange(v, x)
-            z = advance(s, v, p.edge, blank)
+                for v in variables:
+                    for x in (0, 1, lx + 2, lx + 3):
+                        arrange(v, x)
+            packed = advance(s, c, p.edge, [blank] * GROUP)
             if not last:
-                start(x_messages(s + 1, v))
-            z = advance(s, v, p.inner, z)
+                start(x_messages(s + 1, c))
+            packed = advance(s, c, p.inner, packed)
             if last:
-                project(v)
+                for v in variables:
+                    project(v)
                 for i in range(len(partners)):
-                    plane_message(i, v).start()
+                    plane_message(i, pl.ds(c * GROUP, GROUP)).start()
             else:
-                z_out[s + 1, v] = z
-                start(yz_messages(s + 1, v))
+                for v, z in zip(variables, packed):
+                    z_out[s + 1, v] = z
+                start(yz_messages(s + 1, c))
             return carry
 
-        lax.fori_loop(0, nv, stage, 0)
+        lax.fori_loop(0, nv // GROUP, stage, 0)
 
     plane = [plane_message(i, slice(None)) for i in range(len(partners))]
     total = yz_out[my * nz + mz]

time: 31.4 us -> 33.7 us (1.073)
  Pallas kernels: 30.6 us -> 32.9 us
    pallas_call x1, Pallas kernels: 30.6 us -> 32.9 us  [local_kernel(): pl.pallas_call(functools.partial(kernel, p), out_shape=pltpu.VMEM((nv, p....]
where the time goes in v7:
time: 33.7 us; the launch traced here: 33.6 us
  Pallas kernels  32.9 us (98%)
  local copies, waits for them, and re-layouts  0.66 us (2%)
    pallas_call x1, Pallas kernels, local_kernel(): pl.pallas_call(functools.partial(kernel, p), out_shape=pltpu.VMEM((nv, p....  32.9 us

profile of v7, /device:TPU:0, one launch (start us, length us, event | category | flops | bytes accessed | tf_op | source)
XLA Modules:
  0.0 33.6 jit_solution(17311249030309568200)
XLA Ops:
  0.0 32.9 %shard_map.73 = f32[4,8,8,16]{3,2,1,0:T(8,128)S(1)} custom-call(f32[4,8,32,128]{3,2,1,0:T(8,128)} %fields.1, f32[3,8,32,128]{3,2,1,0:T(8,128)} %velocity.1, f32[4]{0:T(128)} %diffusivity_in.1, f32[4,4]{1,0:T(4,128)} %coupling_in.1, f32[8,32]{1,0:T(8,128)} %factor_x_in.1, f32[32,32]{1,0:T(8,128)} %factor_y_in.1, f32[32,128]{1,0:T(8,128)} %bitcast.3), custom_call_target="tpu_custom_call" | custom-call | tf_op jit(solution)/shard_map/pallas_call | solution.py:513
  32.9 0.7 %copy.9 = f32[4,8,16,8]{2,3,1,0:T(8,128)} copy(f32[4,8,16,8]{2,3,1,0:T(8,128)S(1)} %bitcast.2) | data formatting | bytes 32768

commit v8 on v7

--- a/solution.py
+++ b/solution.py
@@ -9,7 +9,7 @@
 STEPS = 2
 STAGES = 2 * STEPS
 HALO = 2
-GROUP = 2
+GROUP = 1
 VMEM_LIMIT = 66 * 1000 * 1000
 MESH = pl.DeviceIdType.MESH
 HIGHEST = lax.Precision.HIGHEST

time: 33.7 us -> 31.4 us (0.932)
  Pallas kernels: 32.9 us -> 30.6 us
    pallas_call x1, Pallas kernels: 32.9 us -> 30.6 us  [local_kernel(): pl.pallas_call(functools.partial(kernel, p), out_shape=pltpu.VMEM((nv, p....]
where the time goes in v8:
time: 31.4 us; the launch traced here: 31.3 us
  Pallas kernels  30.6 us (97%)
  local copies, waits for them, and re-layouts  0.66 us (2%)
    pallas_call x1, Pallas kernels, local_kernel(): pl.pallas_call(functools.partial(kernel, p), out_shape=pltpu.VMEM((nv, p....  30.6 us
    unnamed x1, local copies, waits for them, and re-layouts  0.66 us

profile of v8, /device:TPU:0, one launch (start us, length us, event | category | flops | bytes accessed | tf_op | source)
XLA Modules:
  0.0 31.3 jit_solution(16503731167506012213)
XLA Ops:
  0.0 30.6 %shard_map.73 = f32[4,8,8,16]{3,2,1,0:T(8,128)S(1)} custom-call(f32[4,8,32,128]{3,2,1,0:T(8,128)} %fields.1, f32[3,8,32,128]{3,2,1,0:T(8,128)} %velocity.1, f32[4]{0:T(128)} %diffusivity_in.1, f32[4,4]{1,0:T(4,128)} %coupling_in.1, f32[8,32]{1,0:T(8,128)} %factor_x_in.1, f32[32,32]{1,0:T(8,128)} %factor_y_in.1, f32[32,128]{1,0:T(8,128)} %bitcast.3), custom_call_target="tpu_custom_call" | custom-call | tf_op jit(solution)/shard_map/pallas_call | solution.py:513
  30.6 0.7 %copy.9 = f32[4,8,16,8]{2,3,1,0:T(8,128)} copy(f32[4,8,16,8]{2,3,1,0:T(8,128)S(1)} %bitcast.2) | data formatting | bytes 32768

commit v9 on v8

--- a/solution.py
+++ b/solution.py
@@ -437,41 +437,56 @@
             send_sem=yz_send.at[i], recv_sem=yz_recv.at[i],
             device_id=device, device_id_type=MESH)
 
+    groups = nv // GROUP
+
+    def project(v):
+        state = cells[STAGES, v, 2:lx + 2].reshape(lx * ly, p.lz)
+        reduced = product(split(factor_z[...]), split(state), ((1,), (1,)))
+        reduced = product(split(reduced), (spread_y[0], spread_y[1]))
+        for y in range(ny):
+            for z in range(nz):
+                yz_out[y * nz + z, v] = reduced[
+                    z * p.cz:(z + 1) * p.cz, y * chunk_y:(y + 1) * chunk_y]
+
+    def edge_layers(s, c):
+        variables = [c * GROUP + i for i in range(GROUP)]
+        arrive(yz_messages(s, c) + x_messages(s, c))
+        if s == 0:
+            for v in variables:
+                for x in (0, 1, lx + 2, lx + 3):
+                    arrange(v, x)
+        packed = advance(s, c, p.edge, [blank] * GROUP)
+        if s + 1 < STAGES:
+            start(x_messages(s + 1, c))
+            for v, z in zip(variables, packed):
+                z_out[s + 1, v] = z
+
+    def inner_layers(s, c):
+        variables = [c * GROUP + i for i in range(GROUP)]
+        if s + 1 < STAGES:
+            packed = advance(s, c, p.inner, [z_out[s + 1, v] for v in variables])
+            for v, z in zip(variables, packed):
+                z_out[s + 1, v] = z
+            start(yz_messages(s + 1, c))
+        else:
+            advance(s, c, p.inner, [blank] * GROUP)
+            for v in variables:
+                project(v)
+            for i in range(len(partners)):
+                plane_message(i, pl.ds(c * GROUP, GROUP)).start()
+
     for s in range(STAGES):
-        last = s == STAGES - 1
-
-        def project(v):
-            state = cells[STAGES, v, 2:lx + 2].reshape(lx * ly, p.lz)
-            reduced = product(split(factor_z[...]), split(state), ((1,), (1,)))
-            reduced = product(split(reduced), (spread_y[0], spread_y[1]))
-            for y in range(ny):
-                for z in range(nz):
-                    yz_out[y * nz + z, v] = reduced[
-                        z * p.cz:(z + 1) * p.cz, y * chunk_y:(y + 1) * chunk_y]
+        edge_layers(s, 0)
+        if s > 0:
+            inner_layers(s - 1, groups - 1)
 
         def stage(c, carry):
-            variables = [c * GROUP + i for i in range(GROUP)]
-            arrive(yz_messages(s, c) + x_messages(s, c))
-            if s == 0:
-                for v in variables:
-                    for x in (0, 1, lx + 2, lx + 3):
-                        arrange(v, x)
-            packed = advance(s, c, p.edge, [blank] * GROUP)
-            if not last:
-                start(x_messages(s + 1, c))
-            packed = advance(s, c, p.inner, packed)
-            if last:
-                for v in variables:
-                    project(v)
-                for i in range(len(partners)):
-                    plane_message(i, pl.ds(c * GROUP, GROUP)).start()
-            else:
-                for v, z in zip(variables, packed):
-                    z_out[s + 1, v] = z
-                start(yz_messages(s + 1, c))
+            edge_layers(s, c)
+            inner_layers(s, c - 1)
             return carry
 
-        lax.fori_loop(0, nv // GROUP, stage, 0)
+        lax.fori_loop(1, groups, stage, 0)
+    inner_layers(STAGES - 1, groups - 1)
 
     plane = [plane_message(i, slice(None)) for i in range(len(partners))]
     total = yz_out[my * nz + mz]

time: 31.4 us -> 33.9 us (1.080)
  Pallas kernels: 30.6 us -> 33.1 us
    pallas_call x1, Pallas kernels: 30.6 us -> 33.1 us  [local_kernel(): pl.pallas_call(functools.partial(kernel, p), out_shape=pltpu.VMEM((nv, p....]
where the time goes in v9:
time: 33.9 us; the launch traced here: 33.7 us
  Pallas kernels  33.1 us (98%)
  local copies, waits for them, and re-layouts  0.66 us (2%)
    pallas_call x1, Pallas kernels, local_kernel(): pl.pallas_call(functools.partial(kernel, p), out_shape=pltpu.VMEM((nv, p....  33.1 us

profile of v9, /device:TPU:0, one launch (start us, length us, event | category | flops | bytes accessed | tf_op | source)
XLA Modules:
  0.0 33.7 jit_solution(17943776330196718180)
XLA Ops:
  0.0 33.1 %shard_map.73 = f32[4,8,8,16]{3,2,1,0:T(8,128)S(1)} custom-call(f32[4,8,32,128]{3,2,1,0:T(8,128)} %fields.1, f32[3,8,32,128]{3,2,1,0:T(8,128)} %velocity.1, f32[4]{0:T(128)} %diffusivity_in.1, f32[4,4]{1,0:T(4,128)} %coupling_in.1, f32[8,32]{1,0:T(8,128)} %factor_x_in.1, f32[32,32]{1,0:T(8,128)} %factor_y_in.1, f32[32,128]{1,0:T(8,128)} %bitcast.3), custom_call_target="tpu_custom_call" | custom-call | tf_op jit(solution)/shard_map/pallas_call | solution.py:528
  33.1 0.7 %copy.9 = f32[4,8,16,8]{2,3,1,0:T(8,128)} copy(f32[4,8,16,8]{2,3,1,0:T(8,128)S(1)} %bitcast.2) | data formatting | bytes 32768
